TPU v7x, 32 devices: a whole 2x2x4 slice. The times are simulated.
32 devices in a mesh: rep: 2 (over x), fsdp: 16 (over z, y, core).
Axes of the slice: x: 2, y: 2, z: 4, core: 2. Of those that a mesh axis runs over, the one named last changes fastest.
Arguments:
- activations: bfloat16 [2, 2, 2816, 2560], P('rep', None, 'fsdp'), may hold values from -6 to 6
- residual: bfloat16 [2, 2, 2816, 5120], P('rep', None, 'fsdp'), may hold values from -6 to 6
- upstream: bfloat16 [2, 2, 2816, 5120], P('rep', None, 'fsdp'), may hold values from -6 to 6
- norm_gain: float32 [5120], replicated, may hold values from 0.5 to 1.5
- params: float32 [2, 128, 40, 5, 128], P('rep', 'fsdp'), may hold values from -6 to 6
- momentum: float32 [2, 128, 40, 5, 128], P('rep', 'fsdp'), may hold values from -6 to 6
- pattern: int32 [40, 5], replicated, may hold values from 0 to 19, as said below
- step_index: int32 [1], replicated, may hold values from 0 to 2999
Outputs:
- params_out: float32 [2, 128, 40, 5, 128], P('rep', 'fsdp')
- momentum_out: float32 [2, 128, 40, 5, 128], P('rep', 'fsdp')
Inputs may be any that keep to these rules, and one draw needn't show every extreme that they name: `pattern`: each output block column c lists 5 different input blocks, the first of them c mod 20.
All inputs are finite; a program needn't handle non-finite values.
Results may differ from a plain program's by a relative error of at most 0.012.
Values may be sent and summed in bfloat16 or wider, within the bound.
No kernel may reach another device: no remote copies, remote signals or barrier semaphores. Data moves between devices by JAX's collectives and lax.ppermute only.
A program may use at most 128 MiB of HBM per device.

v0:
```python
import functools
import math
from functools import partial

import jax
import jax.numpy as jnp
import numpy as np
from jax import lax
from jax.experimental import pallas as pl
from jax.experimental.pallas import tpu as pltpu
from jax.sharding import PartitionSpec as P

learn_rate = 0.1
momentum_beta = 0.9
decay_keep = 0.999
epsilon = 1e-06

f32 = jnp.float32
bf16 = jnp.bfloat16
WHOLE = pl.BlockSpec(memory_space=pltpu.VMEM)
SCALARS = pl.BlockSpec(memory_space=pltpu.SMEM)
PARAMS = pltpu.CompilerParams(vmem_limit_bytes=16 * 2**20)


def vmem(x):
    return pltpu.with_memory_space_constraint(x, pltpu.VMEM)


def in_vmem(shape):
    return pltpu.VMEM(shape.shape, shape.dtype)


def after(x, *others):
    if not others:
        return x
    return lax.optimization_barrier((x, *others))[0]


def ring_order(chips):
    if chips % 2:
        return list(range(chips))
    return list(range(0, chips, 2)) + list(range(chips - 1, 0, -2))


def ring_place(chips, chip):
    if chips % 2:
        return chip
    up = lax.div(chip, jnp.int32(2))
    return jnp.where(lax.rem(chip, jnp.int32(2)) == 0, up, chips - 1 - up)


def chip_at(chips, place):
    if chips % 2:
        return place
    return jnp.where(place < chips // 2, 2 * place, 2 * (chips - 1 - place) + 1)


def this_core():
    return lax.rem(lax.axis_index("fsdp"), jnp.int32(2))


class Ring:
    def __init__(self, devices):
        self.chips = devices // 2
        order = ring_order(self.chips)
        n = self.chips
        self.to_right = [
            (2 * order[p] + k, 2 * order[(p + 1) % n] + k) for p in range(n) for k in (0, 1)
        ]
        self.to_left = [(b, a) for a, b in self.to_right]
        self.pair = [(i, i ^ 1) for i in range(devices)]

    def swap(self, x):
        return lax.ppermute(x, "fsdp", self.pair)

    def rounds(self):
        n = self.chips
        short = (n - 1) // 2
        rounds = []
        for s in range(1, n // 2 + 1):
            if s <= n - 1 - short:
                rounds.append([(0, 0, s), (1, 1, s)])
            if s <= short:
                rounds.append([(1, 0, s), (0, 1, s)])
        return rounds

    def move(self, x, direction):
        return lax.ppermute(x, "fsdp", self.to_left if direction else self.to_right)

    def gather(self, halves, beside):
        n = self.chips
        slots = [[x] + [None] * (n - 1) for x in halves]
        arrived = []
        for i, pair in enumerate(self.rounds()):
            ready = beside[i](arrived[i - 3]) if i >= 3 and i in beside else []
            for h, d, s in pair:
                x = after(slots[h][s - 1 if d else (1 - s) % n], *ready)
                slots[h][s if d else n - s] = self.move(x, d)
                ready = []
            arrived.append(slots[pair[0][0]][n - pair[0][2]])
        return slots

    def scatter_sum(self, slots):
        n = self.chips
        moving = {}
        for pair in sorted(self.rounds(), key=lambda pair: -pair[0][2]):
            for h, d, s in pair:
                term = slots[h][n - s if d else s]
                if (h, d) in moving:
                    term = add_low(moving[h, d], term)
                moving[h, d] = self.move(term, d)
        return [
            [slots[h][0]] + [moving[h, d] for d in range(2) if (h, d) in moving]
            for h in range(len(slots))
        ]


def add_kernel(a, b, out):
    out[...] = (a[...].astype(f32) + b[...].astype(f32)).astype(bf16)


def add_low(a, b):
    return pl.pallas_call(
        add_kernel,
        in_specs=[WHOLE, WHOLE],
        out_specs=WHOLE,
        out_shape=in_vmem(a),
        compiler_params=PARAMS,
        cost_estimate=pl.CostEstimate(flops=a.size, bytes_accessed=6 * a.size, transcendentals=0),
        name="add",
    )(vmem(a), vmem(b))


def whole_call(kernel, name, operands, outs, scratch=(), scalars=(), raw=(), cost=(0, 0)):
    return pl.pallas_call(
        kernel,
        in_specs=[SCALARS] * len(scalars)
        + [pl.BlockSpec(memory_space=pl.ANY)] * len(raw)
        + [WHOLE] * len(operands),
        out_specs=[WHOLE] * len(outs),
        out_shape=[in_vmem(x) for x in outs],
        scratch_shapes=list(scratch),
        compiler_params=PARAMS,
        cost_estimate=pl.CostEstimate(flops=cost[0], bytes_accessed=cost[1], transcendentals=0),
        name=name,
    )(
        *scalars,
        *[pltpu.with_memory_space_constraint(x, pltpu.HBM) for x in raw],
        *[vmem(x) for x in operands],
    )


def by_core(body):
    core = this_core()
    for c in range(2):
        pl.when(core == c)(partial(body, c))


def columns_loop(columns, column):
    lax.fori_loop(0, columns, lambda c, _: column(c) or 0, 0, unroll=2 if columns % 2 == 0 else 1)


def halves_of(mine, theirs, core):
    return jnp.concatenate([theirs, mine] if core else [mine, theirs], axis=-2)


def rows_of(x, core):
    rows = x.shape[-2] // 2
    low, high = x[..., :rows, :], x[..., rows:, :]
    return (high, low) if core else (low, high)


def shapes_of(shard):
    half_cols, per_col, rows_in, block = shard
    rows = jax.ShapeDtypeStruct((2 * half_cols, per_col, rows_in // 2, block), f32)
    return rows, jax.ShapeDtypeStruct(shard, bf16)


def merge_kernel(mine, theirs, low_a, low_b):
    half_cols = low_a.shape[0]

    def body(core):
        for h, out in enumerate((low_a, low_b)):

            def column(c, h=h, out=out):
                at = h * half_cols + c
                out[c] = halves_of(mine[at], theirs[at], core).astype(bf16)

            columns_loop(half_cols, column)

    by_core(body)


def merge(mine, theirs, shard):
    low = shapes_of(shard)[1]
    return whole_call(merge_kernel, "merge", [mine, theirs], [low, low], cost=(0, mine.size * 12))


def gathered_sum(parts, c):
    return sum(part[c].astype(f32) for part in parts)


def update_kernel(count, scaling, *refs):
    parts = refs[:count], refs[count : 2 * count]
    moments, weights = refs[2 * count : 2 * count + 2], refs[2 * count + 2 : 2 * count + 4]
    far = refs[2 * count + 4 : 2 * count + 9]
    near, sems = refs[2 * count + 9 : 2 * count + 14], refs[-1]
    moments_out, weights_out, low = near[:2], near[2:4], near[4]
    half_cols = low.shape[0] // 2

    def body(core):
        for h in range(2):

            def column(c, h=h):
                at = h * half_cols + c
                news = []
                for r, gradient in enumerate(rows_of(gathered_sum(parts[h], c), core)):
                    moment = momentum_beta * moments[r][at] + scaling * gradient
                    moments_out[r][at] = moment
                    news.append(decay_keep * weights[r][at] - learn_rate * moment)
                    weights_out[r][at] = news[r]
                low[at] = halves_of(*news, core).astype(bf16)

            columns_loop(half_cols, column)

    by_core(body)
    copies = [pltpu.make_async_copy(near[i], far[i], sems.at[i]) for i in range(5)]
    for copy in copies:
        copy.start()
    for copy in copies:
        copy.wait()


def update(parts, moments, weights, scaling, shard):
    rows = shapes_of(shard)[0]
    low = jax.ShapeDtypeStruct((2 * shard[0], *shard[1:]), bf16)
    outs = [rows] * 4 + [low]
    operands = [*parts[0], *parts[1], *moments, *weights]
    out = pl.pallas_call(
        partial(update_kernel, len(parts[0]), scaling),
        in_specs=[WHOLE] * len(operands),
        out_specs=[pl.BlockSpec(memory_space=pl.ANY)] * 5,
        out_shape=[pltpu.HBM(x.shape, x.dtype) for x in outs],
        scratch_shapes=[pltpu.VMEM(x.shape, x.dtype) for x in outs]
        + [pltpu.SemaphoreType.DMA((5,))],
        compiler_params=PARAMS,
        cost_estimate=pl.CostEstimate(
            flops=rows.size * 20, bytes_accessed=rows.size * 60, transcendentals=0
        ),
        name="update",
    )(*[vmem(x) for x in operands])
    return out[:2], out[2:4], out[4]


def blend_kernel(keep, *refs):
    far, outs, (low_a, low_b) = refs[:3], refs[3:5], refs[5:7]
    near, sems = refs[7:10], refs[10]
    mine, theirs, part = near
    half_cols = low_a.shape[0]
    share = keep[0]
    copies = [pltpu.make_async_copy(far[i], near[i], sems.at[i]) for i in range(3)]
    for copy in copies:
        copy.start()
    for copy in copies:
        copy.wait()

    def body(core):
        for h, low in enumerate((low_a, low_b)):

            def column(c, h=h, low=low):
                at = h * half_cols + c
                news = []
                for own, to, other in zip(
                    (mine, theirs), outs, rows_of(part[at].astype(f32), core)
                ):
                    news.append(share * own[at] + (1.0 - share) * other)
                    to[at] = news[-1]
                low[c] = halves_of(*news, core).astype(bf16)

            columns_loop(half_cols, column)

    by_core(body)


def blend(keep, weights, partner, shard):
    rows, low = shapes_of(shard)
    outs = [rows, rows, low, low]
    raw = pl.BlockSpec(memory_space=pl.ANY)
    out = pl.pallas_call(
        blend_kernel,
        in_specs=[SCALARS] + [raw] * 3,
        out_specs=[WHOLE] * 4,
        out_shape=[in_vmem(x) for x in outs],
        scratch_shapes=[
            pltpu.VMEM(rows.shape, f32),
            pltpu.VMEM(rows.shape, f32),
            pltpu.VMEM(partner.shape, bf16),
            pltpu.SemaphoreType.DMA((3,)),
        ],
        compiler_params=PARAMS,
        cost_estimate=pl.CostEstimate(
            flops=rows.size * 6, bytes_accessed=rows.size * 24, transcendentals=0
        ),
        name="blend",
    )(keep, *[pltpu.with_memory_space_constraint(x, pltpu.HBM) for x in (*weights, partner)])
    return out[:2], list(out[2:])


def last_sum_kernel(count, *refs):
    parts = refs[:count], refs[count : 2 * count]
    outs = refs[2 * count :]
    half_cols = parts[0][0].shape[0]

    def body(core):
        for h in range(2):

            def column(c, h=h):
                for out, rows in zip(outs, rows_of(gathered_sum(parts[h], c), core)):
                    out[h * half_cols + c] = rows

            columns_loop(half_cols, column)

    by_core(body)


def last_sum(parts, shard):
    rows = shapes_of(shard)[0]
    return whole_call(
        partial(last_sum_kernel, len(parts[0])),
        "last_sum",
        [*parts[0], *parts[1]],
        [rows, rows],
        cost=(rows.size * 4, rows.size * 20),
    )


def finish_kernel(scaling, *refs):
    gradients, moments, weights = refs[:2], refs[2:4], refs[4:6]
    outs, near, sems = refs[6:8], refs[8:10], refs[10]
    columns, per_col, rows = gradients[0].shape[:3]
    core = this_core()
    copies = []
    for k in range(per_col):

        def column(c, k=k):
            for side, owner in enumerate((core, 1 - core)):
                at = pl.ds(owner * columns + c, rows, stride=2 * columns)
                moment = momentum_beta * moments[side][c, k] + scaling * gradients[side][c, k]
                near[0][k, at, :] = decay_keep * weights[side][c, k] - learn_rate * moment
                near[1][k, at, :] = moment

        columns_loop(columns, column)
        for i in range(2):
            for r in range(rows):
                rows_of_k = near[i].at[k, pl.ds(r * 2 * columns, 2 * columns)]
                copy = pltpu.make_async_copy(rows_of_k, outs[i].at[r, k], sems.at[i, k])
                copy.start()
                copies.append(copy)
    for copy in copies:
        copy.wait()


def finish(gradients, moments, weights, scaling):
    columns, per_col, rows, block = gradients[0].shape
    operands = [*gradients, *moments, *weights]
    out = pltpu.HBM((rows, per_col, 2 * columns, block), f32)
    weight, moment = pl.pallas_call(
        partial(finish_kernel, scaling),
        in_specs=[WHOLE] * len(operands),
        out_specs=[pl.BlockSpec(memory_space=pl.ANY)] * 2,
        out_shape=[out, out],
        scratch_shapes=[pltpu.VMEM((per_col, rows * 2 * columns, block), f32)] * 2
        + [pltpu.SemaphoreType.DMA((2, per_col))],
        compiler_params=PARAMS,
        cost_estimate=pl.CostEstimate(
            flops=12 * gradients[0].size, bytes_accessed=80 * gradients[0].size, transcendentals=0
        ),
        name="finish",
    )(*[vmem(x) for x in operands])
    return [x.transpose(0, 2, 1, 3) for x in (weight, moment)]


def split_kernel(out_blocks, raw, kept, given, x, sem):
    columns, per_col, rows = kept.shape[:3]
    core = this_core()
    copy = pltpu.make_async_copy(raw, x, sem)
    copy.start()
    copy.wait()

    def column(c):
        for k in range(per_col):
            for out, owner in ((given, 1 - core), (kept, core)):
                start = k * out_blocks + owner * columns + c
                out[c, k] = x[pl.ds(start, rows, stride=per_col * out_blocks), :]

    columns_loop(columns, column)


def split(x):
    rows, out_blocks, per_col, block = x.shape
    flat = x.transpose(0, 2, 1, 3).reshape(-1, block)
    half = jax.ShapeDtypeStruct((out_blocks // 2, per_col, rows, block), f32)
    return whole_call(
        partial(split_kernel, out_blocks),
        "split",
        [],
        [half, half],
        scratch=[pltpu.VMEM(flat.shape, f32), pltpu.SemaphoreType.DMA(())],
        raw=[flat],
        cost=(0, 8 * x.size),
    )


def row_cuts(rows):
    if rows % 16:
        return [pl.ds(0, rows)]
    tiles = rows // 16
    pieces = min(4, tiles)
    edges = [16 * (tiles * i // pieces) for i in range(pieces + 1)]
    return [pl.ds(a, b - a) for a, b in zip(edges, edges[1:])]


def pick_kernel(s, mine, raws, outs, sems):
    core = this_core()
    half = core if mine else 1 - core
    copies = []
    _, rows, wide = outs.shape
    for i, raw in enumerate(raws):
        lanes = pl.ds(0, wide)
        if raw.shape[3] != wide:
            lanes = pl.ds(pl.multiple_of(half * wide, wide), wide)
        for j, cut in enumerate(row_cuts(rows)):
            copies.append(
                pltpu.make_async_copy(raw.at[0, s, cut, lanes], outs.at[i, cut], sems.at[i, j])
            )
    for copy in copies:
        copy.start()
    for copy in copies:
        copy.wait()


def pick(s, mine, wide, *raws):
    rows = raws[0].shape[2]
    count = len(raws)

    def kernel(*refs):
        pick_kernel(s, mine, refs[:count], refs[count], refs[count + 1])

    (out,) = whole_call(
        kernel,
        "pick",
        [],
        [jax.ShapeDtypeStruct((count, rows, wide), bf16)],
        scratch=[pltpu.SemaphoreType.DMA((count, len(row_cuts(rows))))],
        raw=raws,
        cost=(0, 4 * count * rows * wide),
    )
    return out


def turn_kernel(n, scal, own, sib, out, turned):
    in_blocks, block, room = out.shape
    rows = own.shape[1]
    rest = jnp.zeros((room - 2 * rows, block), bf16)
    piece = block // n

    def one(p, carry):
        lane = pl.ds(pl.multiple_of(p * block, block), block)
        x = jnp.concatenate([own[0, :, lane], sib[0, :, lane], rest], axis=0)
        turned[p % 2] = x.T.reshape(n, piece, room)
        for r in range(n):
            out[p, r * piece : (r + 1) * piece] = turned[p % 2, scal[r]]
        return carry

    lax.fori_loop(0, in_blocks, one, 0, unroll=2 if in_blocks % 2 == 0 else 1)


def turn(scal, own, sib, block, n):
    _, rows, features = own.shape
    room = -(-2 * rows // block) * block
    (out,) = whole_call(
        partial(turn_kernel, n),
        "turn",
        [own, sib],
        [jax.ShapeDtypeStruct((features // block, block, room), bf16)],
        scratch=[pltpu.VMEM((2, n, block // n, room), bf16)],
        scalars=[scal],
        cost=(0, 8 * rows * features),
    )
    return out


def forward_kernel(per_col, scaling, n, scal, given, kept, sib, *refs):
    slots = refs[:n], refs[n : 2 * n]
    gain, pre, stats, weight, sums = refs[2 * n :]
    half_cols, _, rows_in, block = slots[0][0].shape
    depth = n * rows_in
    cols = weight.shape[1]
    sums[...] = jnp.zeros_like(sums)
    base = scal[n + 2 * half_cols * per_col]

    for h in range(2):

        def group(i, carry, h=h):
            for r in range(n):
                weight[scal[r]] = slots[h][r][pl.ds(i * cols, cols)]
            for j in range(cols):
                c = h * half_cols + i * cols + j
                lanes = [
                    pl.ds(pl.multiple_of(scal[n + c * per_col + k] * block, block), block)
                    for k in range(per_col)
                ]
                w = jnp.concatenate(
                    [weight[:, j, k].reshape(depth, block) for k in range(per_col)], axis=0
                )
                cut = pl.ds(pl.multiple_of(c * block, block), block)
                sides = ((given, kept, 0), (sib, sib, 1))
                x = jnp.concatenate(
                    [
                        jnp.concatenate([act[0, :, lane] for lane in lanes], axis=1)
                        for act, _, _ in sides
                    ],
                    axis=0,
                )
                proj = scaling * jnp.dot(x, w, preferred_element_type=f32)
                rows = pre.shape[1]
                for t, (_, beside, at) in enumerate(sides):
                    value = beside[at, :, cut].astype(f32) + proj[t * rows : (t + 1) * rows]
                    pre[t, :, cut] = value
                    g = gain[base + c] * beside[at + 1, :, cut].astype(f32)
                    sums[t, 0] += value * value
                    sums[t, 1] += value * g
            return carry

        lax.fori_loop(0, half_cols // cols, group, 0)

    lane = lax.broadcasted_iota(jnp.int32, stats.shape[1:], 1)
    for t in range(2):
        square = jnp.sum(sums[t, 0], axis=1, keepdims=True)
        inner = jnp.sum(sums[t, 1], axis=1, keepdims=True)
        stats[t] = jnp.where(lane < block // 2, square, inner)


def interleaved(main, side):
    done = 0
    for i, step in enumerate(main):
        step()
        upto = len(side) * (i + 1) // len(main)
        for other in side[done:upto]:
            other()
        done = upto


def backward_kernel(per_col, width, n, scal, act_t, pre, kept, sib, gain, own, other, *refs):
    outs = refs[:n], refs[n : 2 * n]
    scales, grad = refs[2 * n :]
    half_cols, _, rows_in, block = outs[0][0].shape
    rows = pre.shape[1]
    cols = grad.shape[1]
    groups = half_cols // cols
    size = 16 if rows % 16 == 0 else rows
    base = scal[n + 2 * half_cols * per_col]

    for t in range(2):
        total = own[t] + other[1 - t]
        square, inner = total[:, 0:1], total[:, block // 2 : block // 2 + 1]
        inv = lax.rsqrt(square / width + epsilon)
        scales[t, 0] = jnp.broadcast_to(inv, scales.shape[2:])
        scales[t, 1] = jnp.broadcast_to(inv * inv * inv * (inner / width), scales.shape[2:])
    for b in range(2):
        grad[b, :, 2 * rows :] = jnp.zeros((cols, grad.shape[2] - 2 * rows, block), bf16)

    def gradients(g, t, at):
        up = sib.at[2] if t else kept.at[1]
        chunk = slice(at, at + size)
        inv, inner = scales[t, 0, chunk], scales[t, 1, chunk]
        for j in range(cols):
            c = g * cols + j
            cut = slice(c * block, (c + 1) * block)
            weighted = gain[base + c] * up[chunk, cut].astype(f32)
            to = slice(t * rows + at, t * rows + at + size)
            grad[g % 2, j, to] = (inv * weighted - pre[t, chunk, cut] * inner).astype(bf16)

    def all_gradients(g):
        if g >= 2 * groups:
            return []
        return [partial(gradients, g, t, at) for t in range(2) for at in range(0, rows, size)]

    def product(g, j):
        at = n + (g * cols + j) * per_col
        x = jnp.concatenate([act_t[scal[at + k]] for k in range(per_col)], axis=0)
        term = jnp.dot(x, grad[g % 2, j], preferred_element_type=f32).astype(bf16)
        term = term.reshape(per_col, n, rows_in, block)
        for r in range(n):
            outs[g // groups][r][g % groups * cols + j] = term[:, r]

    for step in all_gradients(0):
        step()
    for g in range(2 * groups):
        interleaved([partial(product, g, j) for j in range(cols)], all_gradients(g + 1))


def group_columns(half_cols):
    return max(c for c in range(1, 6) if half_cols % c == 0)


def forward(scal, given, kept, sib, slots, gain, scaling):
    n = len(slots[0])
    half_cols, per_col, rows_in, block = slots[0][0].shape
    _, rows, wide = kept.shape
    cols = group_columns(half_cols)
    flops = 4 * rows * wide * per_col * block
    operands = [given, kept, sib, *slots[0], *slots[1], gain]
    return pl.pallas_call(
        partial(forward_kernel, per_col, scaling, n),
        in_specs=[SCALARS] + [WHOLE] * len(operands),
        out_specs=[WHOLE, WHOLE],
        out_shape=[
            in_vmem(jax.ShapeDtypeStruct((2, rows, wide), f32)),
            in_vmem(jax.ShapeDtypeStruct((2, rows, block), f32)),
        ],
        scratch_shapes=[
            pltpu.VMEM((n, cols, per_col, rows_in, block), bf16),
            pltpu.VMEM((2, 2, rows, block), f32),
        ],
        compiler_params=PARAMS,
        cost_estimate=pl.CostEstimate(flops=flops, bytes_accessed=16 * 2**20, transcendentals=0),
        name="forward",
    )(scal, *[vmem(x) for x in operands])


def backward(scal, act_t, pre, kept, sib, gain, own, other, shard, width):
    half_cols, per_col, rows_in, block = shard
    n = block // rows_in
    _, rows, wide = kept.shape
    room = act_t.shape[2]
    cols = group_columns(half_cols)
    flops = 4 * rows * wide * per_col * block
    operands = [act_t, pre, kept, sib, gain, own, other]
    out = pl.pallas_call(
        partial(backward_kernel, per_col, width, n),
        in_specs=[SCALARS] + [WHOLE] * len(operands),
        out_specs=[WHOLE] * (2 * n),
        out_shape=[in_vmem(jax.ShapeDtypeStruct(shard, bf16)) for _ in range(2 * n)],
        scratch_shapes=[
            pltpu.VMEM((2, 2, rows, block), f32),
            pltpu.VMEM((2, cols, room, block), bf16),
        ],
        compiler_params=PARAMS,
        cost_estimate=pl.CostEstimate(flops=flops, bytes_accessed=16 * 2**20, transcendentals=0),
        name="backward",
    )(scal, *[vmem(x) for x in operands])
    return [out[:n], out[n:]]


def gossip_hops():
    devices = lax.axis_size("rep")
    hops = {}
    for entry, stride in enumerate((1, 2, 4)):
        if stride % devices:
            hops.setdefault(stride % devices, []).append(entry)
    return hops


def partner_of(taken, low):
    devices = lax.axis_size("rep")
    partner = None
    for hop, chosen in taken.items():
        shift = [(i, (i + hop) % devices) for i in range(devices)]
        moved = lambda x, last, shift=shift: lax.ppermute(x, "rep", shift)
        if partner is None:
            partner = lax.cond(chosen, moved, lambda x, last: jnp.zeros_like(x), low, 0)
        else:
            partner = lax.cond(chosen, moved, lambda x, last: last, low, partner)
    return low if partner is None else partner


def mixed(taken, weight):
    devices = lax.axis_size("rep")
    for hop, chosen in taken.items():
        shift = [(i, (i + hop) % devices) for i in range(devices)]

        def mean(own, shift=shift):
            return 0.5 * (own + lax.ppermute(own.astype(bf16), "rep", shift).astype(f32))

        weight = lax.cond(chosen, mean, lambda own: own, weight)
    return weight


def body(activations, residual, upstream, norm_gain, params, momentum, pattern, step_index):
    steps, rows, features = activations.shape[1:]
    width = residual.shape[3]
    own_rows, out_blocks, per_col, block = params.shape[1:]
    scaling = 1.0 / math.sqrt(per_col * block)
    ring = Ring(lax.axis_size("fsdp"))
    n = ring.chips
    columns = out_blocks // 2
    half_cols = columns // 2

    core = this_core()
    place = ring_place(n, lax.div(lax.axis_index("fsdp"), jnp.int32(2)))
    places = place + jnp.arange(n, dtype=jnp.int32)
    chips = chip_at(n, jnp.where(places < n, places, places - n))
    used = lax.dynamic_slice_in_dim(pattern, core * columns, columns, 0)
    scal = jnp.concatenate([chips, used.reshape(-1), core[None] * columns]).astype(jnp.int32)
    gain = norm_gain.reshape(out_blocks, 1, block)

    taken, keeps = [], []
    hops = gossip_hops()
    for s in range(steps):
        entry = lax.rem(step_index[0] + s, jnp.int32(3))
        chosen = {hop: [entry == e for e in entries] for hop, entries in hops.items()}
        taken.append({hop: functools.reduce(jnp.logical_or, flags) for hop, flags in chosen.items()})
        moved = functools.reduce(jnp.logical_or, taken[s].values(), jnp.bool_(False))
        keeps.append(jnp.where(moved, 0.5, 1.0).astype(f32).reshape(1))

    shard = (half_cols, per_col, 2 * own_rows, block)
    mine, theirs = split(params[0])
    theirs = ring.swap(theirs)
    weights = [mine, theirs]
    scal, gain, taken, keeps = lax.optimization_barrier((scal, gain, taken, keeps))
    tokens = (activations, residual, upstream)

    def picked(s, mine, arrived):
        arrays = tokens[1:] if mine else tokens
        return pick(s, mine, features, *[after(x, arrived) for x in arrays])

    given = picked(0, False, scal)
    halves = list(merge(*weights, shard))
    halves[0] = after(halves[0], scal)
    sib = ring.swap(after(given, theirs))
    state = {}

    def keep(name, make):
        def work(arrived):
            state[name] = make(arrived)
            return jax.tree.leaves(state[name])

        return work

    for s in range(steps):
        last = s == steps - 1
        beside = {}
        if s == 0:
            beside[3] = keep("moments", lambda arrived: split(after(momentum, arrived)[0]))
        beside[4] = keep("kept", lambda arrived: picked(s, True, arrived))
        if not last:
            beside[5] = keep("later", lambda arrived: picked(s + 1, False, arrived))
        slots = ring.gather(halves, beside)
        for i, work in beside.items():
            if i >= len(ring.rounds()):
                work(halves[0])
        kept = state["kept"]
        act_t = turn(scal, given, sib, block, n)
        pre, own = forward(scal, given, kept, sib, slots, after(gain, act_t), scaling)
        other = ring.swap(own)
        terms = backward(scal, act_t, pre, kept, sib, gain, own, other, shard, float(width))
        ready = []
        if not last:
            given = state["later"]
            sib = ring.swap(after(given, other))
        if s == 0:
            moments = state["moments"]
            moments = [moments[0], ring.swap(after(moments[1], other))]
        if last:
            moments = [moments[0], ring.swap(after(moments[1], other))]
            weights = [weights[0], ring.swap(after(weights[1], other))]
            ready += [moments[1], weights[1]]
        far = n // 2
        terms = [list(t) for t in terms]
        terms[0][far], terms[1][n - far] = lax.optimization_barrier(
            (terms[0][far], terms[1][n - far], *ready)
        )[:2]
        if not last:
            third = max(far - 1, 1)
            terms[0][third] = after(terms[0][third], sib, moments[1])
        parts = ring.scatter_sum(terms)
        if not last:
            moments, weights, low = update(parts, moments, weights, scaling, shard)
            partner = partner_of(after(taken[s], low), low)
            weights, halves = blend(keeps[s], weights, partner, shard)
    mine, theirs = last_sum(parts, shard)
    weight, moment = finish([mine, ring.swap(theirs)], moments, weights, scaling)
    return (mixed(after(taken[-1], weight), weight)[None], moment[None])


def solution(mesh):
    in_specs = (
        P("rep", None, "fsdp", None),
        P("rep", None, "fsdp", None),
        P("rep", None, "fsdp", None),
        P(),
        P("rep", "fsdp", None, None, None),
        P("rep", "fsdp", None, None, None),
        P(),
        P(),
    )
    out_specs = (P("rep", "fsdp", None, None, None), P("rep", "fsdp", None, None, None))
    return jax.shard_map(body, mesh=mesh, in_specs=in_specs, out_specs=out_specs, check_vma=False)
```

profile of v0, /device:TPU:0, one launch (start us, length us, event | category | flops | bytes accessed | tf_op | source)
XLA Modules:
  0.0 189.6 jit_solution(7767461723029459599)
XLA Ops:
  5.7 3.1 %collective-permute-start.3 = (bf16[10,5,16,128]{3,2,1,0:T(8,128)(2,1)S(1)}, bf16[10,5,16,128]{3,2,1,0:T(8,128)(2,1)S(1)}, u32[]{:S(2)}, u32[]{:S(2)}) collective-permute-start(bf16[10,5,16,128]{3,2,1,0:T(8,128)(2,1)S(1)} %get-tuple-element.112.refs_0_), channel_id=1, source_target_pairs={{0,4},{1,5},{4,8},{5,9},{8,12},{9,13},{12,14},{13,15},{14,10},{15,... | collective-permute-start | bytes 614408 | tf_op jit(solution)/shard_map/ppermute | solution.py:88
  10.8 3.8 %collective-permute-done.3.refs_7_ = bf16[10,5,16,128]{3,2,1,0:T(8,128)(2,1)S(1)} collective-permute-done((bf16[10,5,16,128]{3,2,1,0:T(8,128)(2,1)S(1)}, bf16[10,5,16,128]{3,2,1,0:T(8,128)(2,1)S(1)}, u32[]{:S(2)}, u32[]{:S(2)}) %collective-permute-start.3) | collective-permute-done | bytes 204832 | tf_op jit(solution)/shard_map/ppermute | solution.py:88
  14.6 2.1 %collective-permute-start.4 = (bf16[10,5,16,128]{3,2,1,0:T(8,128)(2,1)S(1)}, bf16[10,5,16,128]{3,2,1,0:T(8,128)(2,1)S(1)}, u32[]{:S(2)}, u32[]{:S(2)}) collective-permute-start(bf16[10,5,16,128]{3,2,1,0:T(8,128)(2,1)S(1)} %collective-permute-done.3.refs_7_), channel_id=1, source_target_pairs={{0,4},{1,5},{4,8},{5,9},{8,12},{9,13},{12,14},{13,15},{14,10},{15,... | collective-permute-start | bytes 614408 | tf_op jit(solution)/shard_map/ppermute | solution.py:88
  16.8 2.2 %collective-permute-done.5.refs_15_ = bf16[10,5,16,128]{3,2,1,0:T(8,128)(2,1)S(1)} collective-permute-done((bf16[10,5,16,128]{3,2,1,0:T(8,128)(2,1)S(1)}, bf16[10,5,16,128]{3,2,1,0:T(8,128)(2,1)S(1)}, u32[]{:S(2)}, u32[]{:S(2)}) %collective-permute-start.5) | collective-permute-done | bytes 204832 | tf_op jit(solution)/shard_map/ppermute | solution.py:88
  20.3 2.2 %collective-permute-start.16 = (bf16[10,5,16,128]{3,2,1,0:T(8,128)(2,1)S(1)}, bf16[10,5,16,128]{3,2,1,0:T(8,128)(2,1)S(1)}, u32[]{:S(2)}, u32[]{:S(2)}) collective-permute-start(bf16[10,5,16,128]{3,2,1,0:T(8,128)(2,1)S(1)} %collective-permute-done.5.refs_15_), channel_id=1, source_target_pairs={{0,4},{1,5},{4,8},{5,9},{8,12},{9,13},{12,14},{13,15},{14,10},{15,... | collective-permute-start | bytes 614408 | tf_op jit(solution)/shard_map/ppermute | solution.py:88
  28.3 2.1 %collective-permute-start.17 = (bf16[10,5,16,128]{3,2,1,0:T(8,128)(2,1)S(1)}, bf16[10,5,16,128]{3,2,1,0:T(8,128)(2,1)S(1)}, u32[]{:S(2)}, u32[]{:S(2)}) collective-permute-start(bf16[10,5,16,128]{3,2,1,0:T(8,128)(2,1)S(1)} %collective-permute-done.16.refs_14_), channel_id=1, source_target_pairs={{0,4},{1,5},{4,8},{5,9},{8,12},{9,13},{12,14},{13,15},{14,10},{15,... | collective-permute-start | bytes 614408 | tf_op jit(solution)/shard_map/ppermute | solution.py:88
  32.2 4.3 %collective-permute-done.14.refs_11_ = bf16[10,5,16,128]{3,2,1,0:T(8,128)(2,1)S(1)} collective-permute-done((bf16[10,5,16,128]{3,2,1,0:T(8,128)(2,1)S(1)}, bf16[10,5,16,128]{3,2,1,0:T(8,128)(2,1)S(1)}, u32[]{:S(2)}, u32[]{:S(2)}) %collective-permute-start.14) | collective-permute-done | bytes 204832 | tf_op jit(solution)/shard_map/ppermute | solution.py:88
  42.4 4.3 %forward.2 = (f32[2,176,2560]{2,1,0:T(8,128)S(1)}, f32[2,176,128]{2,1,0:T(8,128)S(1)}) custom-call(s32[109]{0:T(128)S(1)} %pad_add_fusion.scal, bf16[3,176,2560]{2,1,0:T(8,128)(2,1)S(1)} %pick.5.own.given, bf16[2,176,2560]{2,1,0:T(8,128)(2,1)S(1)} %pick.6.kept, bf16[3,176,2560]{2,1,0:T(8,128)(2,1)S(1)} %collective-permute-done.6.sib, ...), custom_call_target="tpu_custom_call" | custom-call | flops 1153433600 | bytes 16777216 | tf_op jit(solution)/shard_map/forward/pallas_call | solution.py:614
  48.6 3.9 %backward.2 = (bf16[10,5,16,128]{3,2,1,0:T(8,128)(2,1)S(1)}, bf16[10,5,16,128]{3,2,1,0:T(8,128)(2,1)S(1)}, bf16[10,5,16,128]{3,2,1,0:T(8,128)(2,1)S(1)}, bf16[10...) custom-call(s32[109]{0:T(128)S(1)} %pad_add_fusion.scal, ...), custom_call_target="tpu_custom_call" | custom-call | flops 1153433600 | bytes 16777216 | tf_op jit(solution)/shard_map/backward/pallas_call | solution.py:640
  56.5 3.9 %collective-permute-done.31.a = bf16[10,5,16,128]{3,2,1,0:T(8,128)(2,1)S(1)} collective-permute-done((bf16[10,5,16,128]{3,2,1,0:T(8,128)(2,1)S(1)}, bf16[10,5,16,128]{3,2,1,0:T(8,128)(2,1)S(1)}, u32[]{:S(2)}, u32[]{:S(2)}) %collective-permute-start.31) | collective-permute-done | bytes 204832 | tf_op jit(solution)/shard_map/ppermute | solution.py:88
  83.7 2.3 %collective-permute-done.30.refs_4_ = bf16[10,5,16,128]{3,2,1,0:T(8,128)(2,1)S(1)} collective-permute-done((bf16[10,5,16,128]{3,2,1,0:T(8,128)(2,1)S(1)}, bf16[10,5,16,128]{3,2,1,0:T(8,128)(2,1)S(1)}, u32[]{:S(2)}, u32[]{:S(2)}) %collective-permute-start.30) | collective-permute-done | bytes 204832 | tf_op jit(solution)/shard_map/ppermute | solution.py:88
  96.4 4.0 %collective-permute-done.39.refs_7_ = bf16[10,5,16,128]{3,2,1,0:T(8,128)(2,1)S(1)} collective-permute-done((bf16[10,5,16,128]{3,2,1,0:T(8,128)(2,1)S(1)}, bf16[10,5,16,128]{3,2,1,0:T(8,128)(2,1)S(1)}, u32[]{:S(2)}, u32[]{:S(2)}) %collective-permute-start.39) | collective-permute-done | bytes 204832 | tf_op jit(solution)/shard_map/ppermute | solution.py:88
  102.4 2.4 %collective-permute-done.35.refs_15_ = bf16[10,5,16,128]{3,2,1,0:T(8,128)(2,1)S(1)} collective-permute-done((bf16[10,5,16,128]{3,2,1,0:T(8,128)(2,1)S(1)}, bf16[10,5,16,128]{3,2,1,0:T(8,128)(2,1)S(1)}, u32[]{:S(2)}, u32[]{:S(2)}) %collective-permute-start.35) | collective-permute-done | bytes 204832 | tf_op jit(solution)/shard_map/ppermute | solution.py:88
  116.4 3.7 %collective-permute-done.45.refs_11_ = bf16[10,5,16,128]{3,2,1,0:T(8,128)(2,1)S(1)} collective-permute-done((bf16[10,5,16,128]{3,2,1,0:T(8,128)(2,1)S(1)}, bf16[10,5,16,128]{3,2,1,0:T(8,128)(2,1)S(1)}, u32[]{:S(2)}, u32[]{:S(2)}) %collective-permute-start.45) | collective-permute-done | bytes 204832 | tf_op jit(solution)/shard_map/ppermute | solution.py:88
  126.6 4.3 %forward.3 = (f32[2,176,2560]{2,1,0:T(8,128)S(1)}, f32[2,176,128]{2,1,0:T(8,128)S(1)}) custom-call(s32[109]{0:T(128)S(1)} %pad_add_fusion.scal, bf16[3,176,2560]{2,1,0:T(8,128)(2,1)S(1)} %pick.4.own.given, bf16[2,176,2560]{2,1,0:T(8,128)(2,1)S(1)} %pick.7.kept, bf16[3,176,2560]{2,1,0:T(8,128)(2,1)S(1)} %copy-done.3, ...), custom_call_target="tpu_custom_call" | custom-call | flops 1153433600 | bytes 16777216 | tf_op jit(solution)/shard_map/forward/pallas_call | solution.py:614
  132.9 3.8 %backward.3 = (bf16[10,5,16,128]{3,2,1,0:T(8,128)(2,1)S(1)}, bf16[10,5,16,128]{3,2,1,0:T(8,128)(2,1)S(1)}, bf16[10,5,16,128]{3,2,1,0:T(8,128)(2,1)S(1)}, bf16[10...) custom-call(s32[109]{0:T(128)S(1)} %pad_add_fusion.scal, ...), custom_call_target="tpu_custom_call" | custom-call | flops 1153433600 | bytes 16777216 | tf_op jit(solution)/shard_map/backward/pallas_call | solution.py:640
  140.8 3.9 %collective-permute-done.52.a = bf16[10,5,16,128]{3,2,1,0:T(8,128)(2,1)S(1)} collective-permute-done((bf16[10,5,16,128]{3,2,1,0:T(8,128)(2,1)S(1)}, bf16[10,5,16,128]{3,2,1,0:T(8,128)(2,1)S(1)}, u32[]{:S(2)}, u32[]{:S(2)}) %collective-permute-start.52) | collective-permute-done | bytes 204832 | tf_op jit(solution)/shard_map/ppermute | solution.py:88
  146.9 3.5 %collective-permute-done.56.a = bf16[10,5,16,128]{3,2,1,0:T(8,128)(2,1)S(1)} collective-permute-done((bf16[10,5,16,128]{3,2,1,0:T(8,128)(2,1)S(1)}, bf16[10,5,16,128]{3,2,1,0:T(8,128)(2,1)S(1)}, u32[]{:S(2)}, u32[]{:S(2)}) %collective-permute-start.56) | collective-permute-done | bytes 204832 | tf_op jit(solution)/shard_map/ppermute | solution.py:88
  155.7 3.5 %collective-permute-done.57.a = bf16[10,5,16,128]{3,2,1,0:T(8,128)(2,1)S(1)} collective-permute-done((bf16[10,5,16,128]{3,2,1,0:T(8,128)(2,1)S(1)}, bf16[10,5,16,128]{3,2,1,0:T(8,128)(2,1)S(1)}, u32[]{:S(2)}, u32[]{:S(2)}) %collective-permute-start.57) | collective-permute-done | bytes 204832 | tf_op jit(solution)/shard_map/ppermute | solution.py:88
  164.7 3.2 %collective-permute-done.58.refs_2_ = bf16[10,5,16,128]{3,2,1,0:T(8,128)(2,1)S(1)} collective-permute-done((bf16[10,5,16,128]{3,2,1,0:T(8,128)(2,1)S(1)}, bf16[10,5,16,128]{3,2,1,0:T(8,128)(2,1)S(1)}, u32[]{:S(2)}, u32[]{:S(2)}) %collective-permute-start.58) | collective-permute-done | bytes 204832 | tf_op jit(solution)/shard_map/ppermute | solution.py:88
  168.0 2.2 %collective-permute-done.55.refs_1_ = bf16[10,5,16,128]{3,2,1,0:T(8,128)(2,1)S(1)} collective-permute-done((bf16[10,5,16,128]{3,2,1,0:T(8,128)(2,1)S(1)}, bf16[10,5,16,128]{3,2,1,0:T(8,128)(2,1)S(1)}, u32[]{:S(2)}, u32[]{:S(2)}) %collective-permute-start.55) | collective-permute-done | bytes 204832 | tf_op jit(solution)/shard_map/ppermute | solution.py:88
  174.7 14.9 %conditional.3 = (f32[8,40,5,128]{3,1,2,0:T(8,128)}) conditional(s32[]{:T(128)} %convert_element_type.13, f32[8,40,5,128]{3,1,2,0:T(8,128)} %bitcast.24, f32[8,40,5,128]{3,1,2,0:T(8,128)} %bitcast.25), branch_computations={%region_2.3_spmd, %region_3.4_spmd} | conditional | flops 819200 | bytes 4915248 | solution.py:686
  177.5 10.0 %collective-permute-done.1 = bf16[8,40,5,128]{3,1,2,0:T(8,128)(2,1)S(1)} collective-permute-done((bf16[8,40,5,128]{3,1,2,0:T(8,128)(2,1)S(1)}, bf16[8,40,5,128]{3,1,2,0:T(8,128)(2,1)S(1)}, u32[]{:S(2)}, u32[]{:S(2)}) %collective-permute-start.1) | collective-permute-done | bytes 409632 | tf_op jit(solution)/shard_map/cond/branch_1_fun/ppermute | solution.py:684
  187.5 2.1 %add_multiply_fusion = f32[8,40,5,128]{3,1,2,0:T(8,128)} fusion(f32[8,40,5,128]{3,1,2,0:T(8,128)} %param.3, bf16[8,40,5,128]{3,1,2,0:T(8,128)(2,1)S(1)} %collective-permute-done.1), kind=kLoop, calls=%fused_computation | loop fusion | flops 614400 | bytes 2048000 | tf_op jit(solution)/shard_map/cond/branch_1_fun/mul | solution.py:684
  (169 shorter events, 108.0 us)
Async XLA Ops:
  5.5 33.0 %collective-permute-start.6 = (bf16[3,176,2560]{2,1,0:T(8,128)(2,1)S(1)}, bf16[3,176,2560]{2,1,0:T(8,128)(2,1)S(1)}, u32[]{:S(2)}, u32[]{:S(2)}) collective-permute-start(bf16[3,176,2560]{2,1,0:T(8,128)(2,1)S(1)} %pick.5.own.given), channel_id=1, source_target_pairs={{0,1},{1,0},{2,3},{3,2},{4,5},{5,4},{6,7},{7,6},{8,9},{9,8},{10,11... | collective-permute-start | bytes 8110088 | tf_op jit(solution)/shard_map/ppermute | solution.py:74
  5.7 8.9 %collective-permute-start.3 = (bf16[10,5,16,128]{3,2,1,0:T(8,128)(2,1)S(1)}, bf16[10,5,16,128]{3,2,1,0:T(8,128)(2,1)S(1)}, u32[]{:S(2)}, u32[]{:S(2)}) collective-permute-start(bf16[10,5,16,128]{3,2,1,0:T(8,128)(2,1)S(1)} %get-tuple-element.112.refs_0_), channel_id=1, source_target_pairs={{0,4},{1,5},{4,8},{5,9},{8,12},{9,13},{12,14},{13,15},{14,10},{15,... | collective-permute-start | bytes 614408 | tf_op jit(solution)/shard_map/ppermute | solution.py:88
  8.8 10.2 %collective-permute-start.5 = (bf16[10,5,16,128]{3,2,1,0:T(8,128)(2,1)S(1)}, bf16[10,5,16,128]{3,2,1,0:T(8,128)(2,1)S(1)}, u32[]{:S(2)}, u32[]{:S(2)}) collective-permute-start(bf16[10,5,16,128]{3,2,1,0:T(8,128)(2,1)S(1)} %get-tuple-element.119.refs_8_), channel_id=1, source_target_pairs={{0,4},{1,5},{4,8},{5,9},{8,12},{9,13},{12,14},{13,15},{14,10},{15,... | collective-permute-start | bytes 614408 | tf_op jit(solution)/shard_map/ppermute | solution.py:88
  10.8 13.3 %collective-permute-start.7 = (bf16[10,5,16,128]{3,2,1,0:T(8,128)(2,1)S(1)}, bf16[10,5,16,128]{3,2,1,0:T(8,128)(2,1)S(1)}, u32[]{:S(2)}, u32[]{:S(2)}) collective-permute-start(bf16[10,5,16,128]{3,2,1,0:T(8,128)(2,1)S(1)} %get-tuple-element.112.refs_0_), channel_id=1, source_target_pairs={{4,0},{5,1},{8,4},{9,5},{12,8},{13,9},{14,12},{15,13},{10,14},{11,... | collective-permute-start | bytes 614408 | tf_op jit(solution)/shard_map/ppermute | solution.py:88
  14.6 9.6 %collective-permute-start.4 = (bf16[10,5,16,128]{3,2,1,0:T(8,128)(2,1)S(1)}, bf16[10,5,16,128]{3,2,1,0:T(8,128)(2,1)S(1)}, u32[]{:S(2)}, u32[]{:S(2)}) collective-permute-start(bf16[10,5,16,128]{3,2,1,0:T(8,128)(2,1)S(1)} %collective-permute-done.3.refs_7_), channel_id=1, source_target_pairs={{0,4},{1,5},{4,8},{5,9},{8,12},{9,13},{12,14},{13,15},{14,10},{15,... | collective-permute-start | bytes 614408 | tf_op jit(solution)/shard_map/ppermute | solution.py:88
  24.3 12.2 %collective-permute-start.14 = (bf16[10,5,16,128]{3,2,1,0:T(8,128)(2,1)S(1)}, bf16[10,5,16,128]{3,2,1,0:T(8,128)(2,1)S(1)}, u32[]{:S(2)}, u32[]{:S(2)}) collective-permute-start(bf16[10,5,16,128]{3,2,1,0:T(8,128)(2,1)S(1)} %collective-permute-done.13.refs_10_), channel_id=1, source_target_pairs={{4,0},{5,1},{8,4},{9,5},{12,8},{13,9},{14,12},{15,13},{10,14},{11,... | collective-permute-start | bytes 614408 | tf_op jit(solution)/shard_map/ppermute | solution.py:88
  26.2 10.4 %collective-permute-start.10 = (bf16[10,5,16,128]{3,2,1,0:T(8,128)(2,1)S(1)}, bf16[10,5,16,128]{3,2,1,0:T(8,128)(2,1)S(1)}, u32[]{:S(2)}, u32[]{:S(2)}) collective-permute-start(bf16[10,5,16,128]{3,2,1,0:T(8,128)(2,1)S(1)} %collective-permute-done.4.refs_6_), channel_id=1, source_target_pairs={{0,4},{1,5},{4,8},{5,9},{8,12},{9,13},{12,14},{13,15},{14,10},{15,... | collective-permute-start | bytes 614408 | tf_op jit(solution)/shard_map/ppermute | solution.py:88
  28.3 12.0 %collective-permute-start.17 = (bf16[10,5,16,128]{3,2,1,0:T(8,128)(2,1)S(1)}, bf16[10,5,16,128]{3,2,1,0:T(8,128)(2,1)S(1)}, u32[]{:S(2)}, u32[]{:S(2)}) collective-permute-start(bf16[10,5,16,128]{3,2,1,0:T(8,128)(2,1)S(1)} %collective-permute-done.16.refs_14_), channel_id=1, source_target_pairs={{0,4},{1,5},{4,8},{5,9},{8,12},{9,13},{12,14},{13,15},{14,10},{15,... | collective-permute-start | bytes 614408 | tf_op jit(solution)/shard_map/ppermute | solution.py:88
  48.1 14.5 %collective-permute-start.19 = (bf16[3,176,2560]{2,1,0:T(8,128)(2,1)S(1)}, bf16[3,176,2560]{2,1,0:T(8,128)(2,1)S(1)}, u32[]{:S(2)}, u32[]{:S(2)}) collective-permute-start(bf16[3,176,2560]{2,1,0:T(8,128)(2,1)S(1)} %pick.4.own.given), channel_id=1, source_target_pairs={{0,1},{1,0},{2,3},{3,2},{4,5},{5,4},{6,7},{7,6},{8,9},{9,8},{10,11... | collective-permute-start | bytes 8110088 | tf_op jit(solution)/shard_map/ppermute | solution.py:74
  48.2 14.2 %collective-permute-start.21 = (f32[20,5,8,128]{3,2,1,0:T(8,128)S(1)}, f32[20,5,8,128]{3,2,1,0:T(8,128)S(1)}, u32[]{:S(2)}, u32[]{:S(2)}) collective-permute-start(f32[20,5,8,128]{3,2,1,0:T(8,128)S(1)} %get-tuple-element.140), channel_id=1, source_target_pairs={{0,1},{1,0},{2,3},{3,2},{4,5},{5,4},{6,7},{7,6},{8,9},{9,8},{10,11... | collective-permute-start | bytes 1228808 | tf_op jit(solution)/shard_map/ppermute | solution.py:74
  54.6 10.3 %collective-permute-start.25 = (bf16[10,5,16,128]{3,2,1,0:T(8,128)(2,1)S(1)}, bf16[10,5,16,128]{3,2,1,0:T(8,128)(2,1)S(1)}, u32[]{:S(2)}, u32[]{:S(2)}) collective-permute-start(bf16[10,5,16,128]{3,2,1,0:T(8,128)(2,1)S(1)} %get-tuple-element.144), channel_id=1, source_target_pairs={{4,0},{5,1},{8,4},{9,5},{12,8},{13,9},{14,12},{15,13},{10,14},{11,... | collective-permute-start | bytes 614408 | tf_op jit(solution)/shard_map/ppermute | solution.py:88
  62.7 10.2 %collective-permute-start.22 = (bf16[10,5,16,128]{3,2,1,0:T(8,128)(2,1)S(1)}, bf16[10,5,16,128]{3,2,1,0:T(8,128)(2,1)S(1)}, u32[]{:S(2)}, u32[]{:S(2)}) collective-permute-start(bf16[10,5,16,128]{3,2,1,0:T(8,128)(2,1)S(1)} %add.53), channel_id=1, source_target_pairs={{0,4},{1,5},{4,8},{5,9},{8,12},{9,13},{12,14},{13,15},{14,10},{15,... | collective-permute-start | bytes 614408 | tf_op jit(solution)/shard_map/ppermute | solution.py:88
  64.9 10.0 %collective-permute-start.26 = (bf16[10,5,16,128]{3,2,1,0:T(8,128)(2,1)S(1)}, bf16[10,5,16,128]{3,2,1,0:T(8,128)(2,1)S(1)}, u32[]{:S(2)}, u32[]{:S(2)}) collective-permute-start(bf16[10,5,16,128]{3,2,1,0:T(8,128)(2,1)S(1)} %add.56), channel_id=1, source_target_pairs={{4,0},{5,1},{8,4},{9,5},{12,8},{13,9},{14,12},{15,13},{10,14},{11,... | collective-permute-start | bytes 614408 | tf_op jit(solution)/shard_map/ppermute | solution.py:88
  94.3 10.4 %collective-permute-start.35 = (bf16[10,5,16,128]{3,2,1,0:T(8,128)(2,1)S(1)}, bf16[10,5,16,128]{3,2,1,0:T(8,128)(2,1)S(1)}, u32[]{:S(2)}, u32[]{:S(2)}) collective-permute-start(bf16[10,5,16,128]{3,2,1,0:T(8,128)(2,1)S(1)} %get-tuple-element.160.refs_8_), channel_id=1, source_target_pairs={{0,4},{1,5},{4,8},{5,9},{8,12},{9,13},{12,14},{13,15},{14,10},{15,... | collective-permute-start | bytes 614408 | tf_op jit(solution)/shard_map/ppermute | solution.py:88
  95.9 12.0 %collective-permute-start.36 = (bf16[10,5,16,128]{3,2,1,0:T(8,128)(2,1)S(1)}, bf16[10,5,16,128]{3,2,1,0:T(8,128)(2,1)S(1)}, u32[]{:S(2)}, u32[]{:S(2)}) collective-permute-start(bf16[10,5,16,128]{3,2,1,0:T(8,128)(2,1)S(1)} %get-tuple-element.163.refs_0_), channel_id=1, source_target_pairs={{4,0},{5,1},{8,4},{9,5},{12,8},{13,9},{14,12},{15,13},{10,14},{11,... | collective-permute-start | bytes 614408 | tf_op jit(solution)/shard_map/ppermute | solution.py:88
  100.3 8.8 %collective-permute-start.40 = (bf16[10,5,16,128]{3,2,1,0:T(8,128)(2,1)S(1)}, bf16[10,5,16,128]{3,2,1,0:T(8,128)(2,1)S(1)}, u32[]{:S(2)}, u32[]{:S(2)}) collective-permute-start(bf16[10,5,16,128]{3,2,1,0:T(8,128)(2,1)S(1)} %collective-permute-done.39.refs_7_), channel_id=1, source_target_pairs={{0,4},{1,5},{4,8},{5,9},{8,12},{9,13},{12,14},{13,15},{14,10},{15,... | collective-permute-start | bytes 614408 | tf_op jit(solution)/shard_map/ppermute | solution.py:88
  110.3 9.8 %collective-permute-start.45 = (bf16[10,5,16,128]{3,2,1,0:T(8,128)(2,1)S(1)}, bf16[10,5,16,128]{3,2,1,0:T(8,128)(2,1)S(1)}, u32[]{:S(2)}, u32[]{:S(2)}) collective-permute-start(bf16[10,5,16,128]{3,2,1,0:T(8,128)(2,1)S(1)} %collective-permute-done.44.refs_10_), channel_id=1, source_target_pairs={{4,0},{5,1},{8,4},{9,5},{12,8},{13,9},{14,12},{15,13},{10,14},{11,... | collective-permute-start | bytes 614408 | tf_op jit(solution)/shard_map/ppermute | solution.py:88
  110.8 10.0 %collective-permute-start.41 = (bf16[10,5,16,128]{3,2,1,0:T(8,128)(2,1)S(1)}, bf16[10,5,16,128]{3,2,1,0:T(8,128)(2,1)S(1)}, u32[]{:S(2)}, u32[]{:S(2)}) collective-permute-start(bf16[10,5,16,128]{3,2,1,0:T(8,128)(2,1)S(1)} %collective-permute-done.40.refs_6_), channel_id=1, source_target_pairs={{0,4},{1,5},{4,8},{5,9},{8,12},{9,13},{12,14},{13,15},{14,10},{15,... | collective-permute-start | bytes 614408 | tf_op jit(solution)/shard_map/ppermute | solution.py:88
  114.4 9.5 %collective-permute-start.48 = (bf16[10,5,16,128]{3,2,1,0:T(8,128)(2,1)S(1)}, bf16[10,5,16,128]{3,2,1,0:T(8,128)(2,1)S(1)}, u32[]{:S(2)}, u32[]{:S(2)}) collective-permute-start(bf16[10,5,16,128]{3,2,1,0:T(8,128)(2,1)S(1)} %collective-permute-done.47.refs_14_), channel_id=1, source_target_pairs={{0,4},{1,5},{4,8},{5,9},{8,12},{9,13},{12,14},{13,15},{14,10},{15,... | collective-permute-start | bytes 614408 | tf_op jit(solution)/shard_map/ppermute | solution.py:88
  138.8 11.6 %collective-permute-start.56 = (bf16[10,5,16,128]{3,2,1,0:T(8,128)(2,1)S(1)}, bf16[10,5,16,128]{3,2,1,0:T(8,128)(2,1)S(1)}, u32[]{:S(2)}, u32[]{:S(2)}) collective-permute-start(bf16[10,5,16,128]{3,2,1,0:T(8,128)(2,1)S(1)} %get-tuple-element.179), channel_id=1, source_target_pairs={{4,0},{5,1},{8,4},{9,5},{12,8},{13,9},{14,12},{15,13},{10,14},{11,... | collective-permute-start | bytes 614408 | tf_op jit(solution)/shard_map/ppermute | solution.py:88
  140.2 11.1 %collective-permute-start.59 = (bf16[10,5,16,128]{3,2,1,0:T(8,128)(2,1)S(1)}, bf16[10,5,16,128]{3,2,1,0:T(8,128)(2,1)S(1)}, u32[]{:S(2)}, u32[]{:S(2)}) collective-permute-start(bf16[10,5,16,128]{3,2,1,0:T(8,128)(2,1)S(1)} %get-tuple-element.183), channel_id=1, source_target_pairs={{0,4},{1,5},{4,8},{5,9},{8,12},{9,13},{12,14},{13,15},{14,10},{15,... | collective-permute-start | bytes 614408 | tf_op jit(solution)/shard_map/ppermute | solution.py:88
  153.5 9.0 %collective-permute-start.54 = (bf16[10,5,16,128]{3,2,1,0:T(8,128)(2,1)S(1)}, bf16[10,5,16,128]{3,2,1,0:T(8,128)(2,1)S(1)}, u32[]{:S(2)}, u32[]{:S(2)}) collective-permute-start(bf16[10,5,16,128]{3,2,1,0:T(8,128)(2,1)S(1)} %add.64), channel_id=1, source_target_pairs={{0,4},{1,5},{4,8},{5,9},{8,12},{9,13},{12,14},{13,15},{14,10},{15,... | collective-permute-start | bytes 614408 | tf_op jit(solution)/shard_map/ppermute | solution.py:88
  154.9 9.0 %collective-permute-start.64 = (bf16[10,5,16,128]{3,2,1,0:T(8,128)(2,1)S(1)}, bf16[10,5,16,128]{3,2,1,0:T(8,128)(2,1)S(1)}, u32[]{:S(2)}, u32[]{:S(2)}) collective-permute-start(bf16[10,5,16,128]{3,2,1,0:T(8,128)(2,1)S(1)} %add.71), channel_id=1, source_target_pairs={{4,0},{5,1},{8,4},{9,5},{12,8},{13,9},{14,12},{15,13},{10,14},{11,... | collective-permute-start | bytes 614408 | tf_op jit(solution)/shard_map/ppermute | solution.py:88
  175.9 11.6 %collective-permute-start.1 = (bf16[8,40,5,128]{3,1,2,0:T(8,128)(2,1)S(1)}, bf16[8,40,5,128]{3,1,2,0:T(8,128)(2,1)S(1)}, u32[]{:S(2)}, u32[]{:S(2)}) collective-permute-start(bf16[8,40,5,128]{3,1,2,0:T(8,128)(2,1)S(1)} %convert_element_type.8), channel_id=1, source_target_pairs={{0,16},{16,0},{1,17},{17,1},{2,18},{18,2},{3,19},{19,3},{4,20},{20... | collective-permute-start | bytes 1228808 | tf_op jit(solution)/shard_map/cond/branch_1_fun/ppermute | solution.py:684
  (49 other events, 410.7 us)
where the time goes:
time: 190 us
  waiting for transfers between devices  79.5 us (42%)
  starting transfers between devices  68.5 us (36%)
  Pallas kernels  35.3 us (19%)
  other arithmetic  3.42 us (2%)
    ppermute x56, starting transfers between devices, move(): return lax.ppermute(x, 'fsdp', self.to_left if direction else self.to_right)  65 us
    ppermute x56, waiting for transfers between devices, move(): return lax.ppermute(x, 'fsdp', self.to_left if direction else self.to_right)  64.9 us
    pallas_call x10, Pallas kernels, whole_call(): pl.pallas_call(kernel, in_specs=[SCALARS] * len(scalars) + [pl.BlockSpec(...  13.5 us
    ppermute x1, waiting for transfers between devices, mean(): lax.ppermute(own.astype(bf16), 'rep', shift).astype(f32)  10 us
    pallas_call x2, Pallas kernels, forward(): pl.pallas_call(partial(forward_kernel, per_col, scaling, n), in_specs=[SC...  8.54 us
    pallas_call x2, Pallas kernels, backward(): pl.pallas_call(partial(backward_kernel, per_col, width, n), in_specs=[SCA...  7.7 us
    ppermute x9, waiting for transfers between devices, swap(): return lax.ppermute(x, 'fsdp', self.pair)  4.56 us
  transfers between devices with their start and end apart: 66, of which 36 were waited for; matrix products, arithmetic and copies ran while one was open for 0% of the time, Pallas kernels for 11%

commit v1 on v0

--- a/solution.py
+++ b/solution.py
@@ -92,7 +92,7 @@
         slots = [[x] + [None] * (n - 1) for x in halves]
         arrived = []
         for i, pair in enumerate(self.rounds()):
-            ready = beside[i](arrived[i - 3]) if i >= 3 and i in beside else []
+            ready = beside[i](arrived[i - 3] if i >= 3 else halves[0]) if i in beside else []
             for h, d, s in pair:
                 x = after(slots[h][s - 1 if d else (1 - s) % n], *ready)
                 slots[h][s if d else n - s] = self.move(x, d)
@@ -490,55 +490,53 @@
     return out
 
 
-def forward_kernel(per_col, scaling, n, scal, given, kept, sib, *refs):
-    slots = refs[:n], refs[n : 2 * n]
-    gain, pre, stats, weight, sums = refs[2 * n :]
-    half_cols, _, rows_in, block = slots[0][0].shape
-    depth = n * rows_in
-    cols = weight.shape[1]
-    sums[...] = jnp.zeros_like(sums)
-    base = scal[n + 2 * half_cols * per_col]
+def far_slots(n):
+    return n // 2, n - n // 2
+
+
+def features_of(act_t, scal, n, at, per_col, slots):
+    piece = act_t.shape[1] // n
+    runs = []
+    for r in slots:
+        if runs and runs[-1][1] == r * piece:
+            runs[-1][1] += piece
+        else:
+            runs.append([r * piece, (r + 1) * piece])
+    return jnp.concatenate(
+        [act_t[scal[n + at * per_col + k], a:b] for k in range(per_col) for a, b in runs], axis=0
+    )
+
+
+def project(act_t, scal, n, at, weights, j):
+    per_col = weights[min(weights)].shape[1]
+    x = features_of(act_t, scal, n, at, per_col, sorted(weights))
+    w = jnp.concatenate(
+        [weights[r][j, k] for k in range(per_col) for r in sorted(weights)], axis=0
+    )
+    return lax.dot_general(x, w, (((0,), (0,)), ((), ())), preferred_element_type=f32)
+
+
+def forward_kernel(scaling, n, scal, act_t, kept, sib, *refs):
+    near = [[r for r in range(n) if r != f] for f in far_slots(n)]
+    slots = [dict(zip(near[0], refs)), dict(zip(near[1], refs[n - 1 :]))]
+    part = refs[-1]
+    half_cols, _, _, block = refs[0].shape
+    rows = part.shape[1]
+    cols = group_columns(half_cols)
 
     for h in range(2):
 
         def group(i, carry, h=h):
-            for r in range(n):
-                weight[scal[r]] = slots[h][r][pl.ds(i * cols, cols)]
             for j in range(cols):
                 c = h * half_cols + i * cols + j
-                lanes = [
-                    pl.ds(pl.multiple_of(scal[n + c * per_col + k] * block, block), block)
-                    for k in range(per_col)
-                ]
-                w = jnp.concatenate(
-                    [weight[:, j, k].reshape(depth, block) for k in range(per_col)], axis=0
-                )
                 cut = pl.ds(pl.multiple_of(c * block, block), block)
-                sides = ((given, kept, 0), (sib, sib, 1))
-                x = jnp.concatenate(
-                    [
-                        jnp.concatenate([act[0, :, lane] for lane in lanes], axis=1)
-                        for act, _, _ in sides
-                    ],
-                    axis=0,
-                )
-                proj = scaling * jnp.dot(x, w, preferred_element_type=f32)
-                rows = pre.shape[1]
-                for t, (_, beside, at) in enumerate(sides):
-                    value = beside[at, :, cut].astype(f32) + proj[t * rows : (t + 1) * rows]
-                    pre[t, :, cut] = value
-                    g = gain[base + c] * beside[at + 1, :, cut].astype(f32)
-                    sums[t, 0] += value * value
-                    sums[t, 1] += value * g
+                out = scaling * project(act_t, scal, n, c, slots[h], i * cols + j)
+                for t, res in enumerate((kept.at[0], sib.at[1])):
+                    value = res[:, cut].astype(f32) + out[t * rows : (t + 1) * rows]
+                    part[t, :, cut] = value
             return carry
 
         lax.fori_loop(0, half_cols // cols, group, 0)
-
-    lane = lax.broadcasted_iota(jnp.int32, stats.shape[1:], 1)
-    for t in range(2):
-        square = jnp.sum(sums[t, 0], axis=1, keepdims=True)
-        inner = jnp.sum(sums[t, 1], axis=1, keepdims=True)
-        stats[t] = jnp.where(lane < block // 2, square, inner)
 
 
 def interleaved(main, side):
@@ -551,13 +549,55 @@
         done = upto
 
 
+def norm_kernel(per_col, scaling, n, scal, act_t, part, kept, sib, gain, far_a, far_b, *refs):
+    pre, stats, sums, share = refs
+    half_cols, _, _, block = far_a.shape
+    rows = pre.shape[1]
+    cols = group_columns(half_cols)
+    base = scal[n + 2 * half_cols * per_col]
+    sums[...] = jnp.zeros_like(sums)
+
+    size = 16 if rows % 16 == 0 else rows
+
+    def product(c):
+        h = c // half_cols
+        f, far = far_slots(n)[h], (far_a, far_b)[h]
+        share[c // cols % 2, c % cols] = project(act_t, scal, n, c, {f: far}, c % half_cols)
+
+    def add_up(g, t, at):
+        chunk = slice(at, at + size)
+        square, inner = sums[t, 0, chunk], sums[t, 1, chunk]
+        for j in range(cols):
+            c = g * cols + j
+            cut = slice(c * block, (c + 1) * block)
+            own = share[g % 2, j, t * rows + at : t * rows + at + size]
+            value = part[t, chunk, cut] + scaling * own
+            pre[t, chunk, cut] = value
+            up = (sib.at[2] if t else kept.at[1])[chunk, cut].astype(f32)
+            square += value * value
+            inner += value * (gain[base + c] * up)
+        sums[t, 0, chunk], sums[t, 1, chunk] = square, inner
+
+    groups = 2 * half_cols // cols
+    for g in range(groups + 1):
+        side = []
+        if g > 0:
+            side = [partial(add_up, g - 1, t, at) for t in range(2) for at in range(0, rows, size)]
+        main = [partial(product, c) for c in range(g * cols, (g + 1) * cols) if g < groups]
+        interleaved(main or [lambda: None], side)
+
+    lane = lax.broadcasted_iota(jnp.int32, stats.shape[1:], 1)
+    for t in range(2):
+        square = jnp.sum(sums[t, 0], axis=1, keepdims=True)
+        inner = jnp.sum(sums[t, 1], axis=1, keepdims=True)
+        stats[t] = jnp.where(lane < block // 2, square, inner)
+
+
 def backward_kernel(per_col, width, n, scal, act_t, pre, kept, sib, gain, own, other, *refs):
-    outs = refs[:n], refs[n : 2 * n]
-    scales, grad = refs[2 * n :]
-    half_cols, _, rows_in, block = outs[0][0].shape
+    outs, grad, scales = refs[:2], refs[2], refs[3]
+    half_cols, _, rows_in, block = outs[0].shape
     rows = pre.shape[1]
-    cols = grad.shape[1]
-    groups = half_cols // cols
+    cols = group_columns(half_cols)
     size = 16 if rows % 16 == 0 else rows
     base = scal[n + 2 * half_cols * per_col]
 
@@ -567,90 +607,119 @@
         inv = lax.rsqrt(square / width + epsilon)
         scales[t, 0] = jnp.broadcast_to(inv, scales.shape[2:])
         scales[t, 1] = jnp.broadcast_to(inv * inv * inv * (inner / width), scales.shape[2:])
-    for b in range(2):
-        grad[b, :, 2 * rows :] = jnp.zeros((cols, grad.shape[2] - 2 * rows, block), bf16)
+    grad[:, 2 * rows :] = jnp.zeros((2 * half_cols, grad.shape[1] - 2 * rows, block), bf16)
 
     def gradients(g, t, at):
         up = sib.at[2] if t else kept.at[1]
         chunk = slice(at, at + size)
         inv, inner = scales[t, 0, chunk], scales[t, 1, chunk]
-        for j in range(cols):
-            c = g * cols + j
+        for c in range(g * cols, (g + 1) * cols):
             cut = slice(c * block, (c + 1) * block)
             weighted = gain[base + c] * up[chunk, cut].astype(f32)
             to = slice(t * rows + at, t * rows + at + size)
-            grad[g % 2, j, to] = (inv * weighted - pre[t, chunk, cut] * inner).astype(bf16)
-
-    def all_gradients(g):
-        if g >= 2 * groups:
-            return []
-        return [partial(gradients, g, t, at) for t in range(2) for at in range(0, rows, size)]
-
-    def product(g, j):
-        at = n + (g * cols + j) * per_col
-        x = jnp.concatenate([act_t[scal[at + k]] for k in range(per_col)], axis=0)
-        term = jnp.dot(x, grad[g % 2, j], preferred_element_type=f32).astype(bf16)
-        term = term.reshape(per_col, n, rows_in, block)
-        for r in range(n):
-            outs[g // groups][r][g % groups * cols + j] = term[:, r]
-
-    for step in all_gradients(0):
-        step()
-    for g in range(2 * groups):
-        interleaved([partial(product, g, j) for j in range(cols)], all_gradients(g + 1))
+            grad[c, to] = (inv * weighted - pre[t, chunk, cut] * inner).astype(bf16)
+
+    def product(c):
+        h = c // half_cols
+        x = features_of(act_t, scal, n, c, per_col, [far_slots(n)[h]])
+        term = jnp.dot(x, grad[c], preferred_element_type=f32).astype(bf16)
+        outs[h][c % half_cols] = term.reshape(per_col, rows_in, block)
+
+    groups = 2 * half_cols // cols
+    for g in range(groups + 1):
+        side = []
+        if g < groups:
+            side = [partial(gradients, g, t, at) for t in range(2) for at in range(0, rows, size)]
+        main = [partial(product, c) for c in range(max(g - 1, 0) * cols, g * cols)]
+        interleaved(main or [lambda: None], side)
+
+
+def terms_kernel(per_col, n, scal, act_t, grad, *outs):
+    near = [[r for r in range(n) if r != f] for f in far_slots(n)]
+    outs = [dict(zip(near[0], outs)), dict(zip(near[1], outs[n - 1 :]))]
+    half_cols, _, rows_in, block = outs[0][near[0][0]].shape
+    for c in range(2 * half_cols):
+        h, at = c // half_cols, c % half_cols
+        x = features_of(act_t, scal, n, c, per_col, range(n))
+        term = jnp.dot(x, grad[c], preferred_element_type=f32)
+        term = term.astype(bf16).reshape(per_col, n, rows_in, block)
+        for r in near[h]:
+            outs[h][r][at] = term[:, r]
 
 
 def group_columns(half_cols):
     return max(c for c in range(1, 6) if half_cols % c == 0)
 
 
-def forward(scal, given, kept, sib, slots, gain, scaling):
+def forward(scal, act_t, kept, sib, slots, scaling):
     n = len(slots[0])
     half_cols, per_col, rows_in, block = slots[0][0].shape
     _, rows, wide = kept.shape
-    cols = group_columns(half_cols)
-    flops = 4 * rows * wide * per_col * block
-    operands = [given, kept, sib, *slots[0], *slots[1], gain]
-    return pl.pallas_call(
-        partial(forward_kernel, per_col, scaling, n),
-        in_specs=[SCALARS] + [WHOLE] * len(operands),
-        out_specs=[WHOLE, WHOLE],
-        out_shape=[
-            in_vmem(jax.ShapeDtypeStruct((2, rows, wide), f32)),
-            in_vmem(jax.ShapeDtypeStruct((2, rows, block), f32)),
+    near = [x for h, f in enumerate(far_slots(n)) for r, x in enumerate(slots[h]) if r != f]
+    (part,) = whole_call(
+        partial(forward_kernel, scaling, n),
+        "forward",
+        [act_t, kept, sib, *near],
+        [jax.ShapeDtypeStruct((2, rows, wide), f32)],
+        scalars=[scal],
+        cost=(4 * rows * wide * per_col * block, 16 * 2**20),
+    )
+    return part
+
+
+def norm(scal, act_t, part, kept, sib, gain, slots, scaling):
+    n = len(slots[0])
+    half_cols, per_col, rows_in, block = slots[0][0].shape
+    _, rows, wide = part.shape
+    far = [slots[h][f] for h, f in enumerate(far_slots(n))]
+    return whole_call(
+        partial(norm_kernel, per_col, scaling, n),
+        "norm",
+        [act_t, part, kept, sib, gain, *far],
+        [jax.ShapeDtypeStruct(part.shape, f32), jax.ShapeDtypeStruct((2, rows, block), f32)],
+        scratch=[
+            pltpu.VMEM((2, 2, rows, block), f32),
+            pltpu.VMEM((2, group_columns(half_cols), act_t.shape[2], block), f32),
         ],
-        scratch_shapes=[
-            pltpu.VMEM((n, cols, per_col, rows_in, block), bf16),
-            pltpu.VMEM((2, 2, rows, block), f32),
-        ],
-        compiler_params=PARAMS,
-        cost_estimate=pl.CostEstimate(flops=flops, bytes_accessed=16 * 2**20, transcendentals=0),
-        name="forward",
-    )(scal, *[vmem(x) for x in operands])
+        scalars=[scal],
+        cost=(4 * rows * wide * per_col * rows_in, 16 * 2**20),
+    )
 
 
 def backward(scal, act_t, pre, kept, sib, gain, own, other, shard, width):
     half_cols, per_col, rows_in, block = shard
     n = block // rows_in
-    _, rows, wide = kept.shape
-    room = act_t.shape[2]
-    cols = group_columns(half_cols)
-    flops = 4 * rows * wide * per_col * block
-    operands = [act_t, pre, kept, sib, gain, own, other]
-    out = pl.pallas_call(
+    rows, wide = pre.shape[1:]
+    term = jax.ShapeDtypeStruct(shard, bf16)
+    grad = jax.ShapeDtypeStruct((2 * half_cols, act_t.shape[2], block), bf16)
+    *far, grad = whole_call(
         partial(backward_kernel, per_col, width, n),
-        in_specs=[SCALARS] + [WHOLE] * len(operands),
-        out_specs=[WHOLE] * (2 * n),
-        out_shape=[in_vmem(jax.ShapeDtypeStruct(shard, bf16)) for _ in range(2 * n)],
-        scratch_shapes=[
-            pltpu.VMEM((2, 2, rows, block), f32),
-            pltpu.VMEM((2, cols, room, block), bf16),
-        ],
-        compiler_params=PARAMS,
-        cost_estimate=pl.CostEstimate(flops=flops, bytes_accessed=16 * 2**20, transcendentals=0),
-        name="backward",
-    )(scal, *[vmem(x) for x in operands])
-    return [out[:n], out[n:]]
+        "backward",
+        [act_t, pre, kept, sib, gain, own, other],
+        [term, term, grad],
+        scratch=[pltpu.VMEM((2, 2, rows, block), f32)],
+        scalars=[scal],
+        cost=(4 * rows * wide * per_col * rows_in, 16 * 2**20),
+    )
+    return far, grad
+
+
+def other_terms(scal, act_t, grad, far, shard):
+    half_cols, per_col, rows_in, block = shard
+    n = block // rows_in
+    near = whole_call(
+        partial(terms_kernel, per_col, n),
+        "terms",
+        [act_t, grad],
+        [jax.ShapeDtypeStruct(shard, bf16)] * (2 * n - 2),
+        scalars=[scal],
+        cost=(2 * grad.size * per_col * block, 16 * 2**20),
+    )
+    slots = []
+    for h, f in enumerate(far_slots(n)):
+        mine = list(near[h * (n - 1) : (h + 1) * (n - 1)])
+        slots.append(mine[:f] + [far[h]] + mine[f:])
+    return slots
 
 
 def gossip_hops():
@@ -740,39 +809,37 @@
 
     for s in range(steps):
         last = s == steps - 1
-        beside = {}
-        if s == 0:
-            beside[3] = keep("moments", lambda arrived: split(after(momentum, arrived)[0]))
-        beside[4] = keep("kept", lambda arrived: picked(s, True, arrived))
+        beside = {2: keep("kept", lambda arrived: picked(s, True, arrived))}
         if not last:
-            beside[5] = keep("later", lambda arrived: picked(s + 1, False, arrived))
+            beside[3] = keep("later", lambda arrived: picked(s + 1, False, arrived))
+        beside[4] = keep("turned", lambda arrived: turn(after(scal, arrived), given, sib, block, n))
         slots = ring.gather(halves, beside)
         for i, work in beside.items():
             if i >= len(ring.rounds()):
                 work(halves[0])
-        kept = state["kept"]
-        act_t = turn(scal, given, sib, block, n)
-        pre, own = forward(scal, given, kept, sib, slots, after(gain, act_t), scaling)
+        kept, act_t = state["kept"], state["turned"]
+        part = forward(scal, act_t, kept, sib, slots, scaling)
+        pre, own = norm(scal, act_t, part, kept, sib, gain, slots, scaling)
         other = ring.swap(own)
-        terms = backward(scal, act_t, pre, kept, sib, gain, own, other, shard, float(width))
+        if s == 0:
+            moments = split(after(momentum, own)[0])
+            other = after(other, *moments)
+        first, grad = backward(scal, act_t, pre, kept, sib, gain, own, other, shard, float(width))
         ready = []
         if not last:
             given = state["later"]
             sib = ring.swap(after(given, other))
         if s == 0:
-            moments = state["moments"]
             moments = [moments[0], ring.swap(after(moments[1], other))]
         if last:
             moments = [moments[0], ring.swap(after(moments[1], other))]
             weights = [weights[0], ring.swap(after(weights[1], other))]
             ready += [moments[1], weights[1]]
-        far = n // 2
-        terms = [list(t) for t in terms]
-        terms[0][far], terms[1][n - far] = lax.optimization_barrier(
-            (terms[0][far], terms[1][n - far], *ready)
-        )[:2]
+        if ready:
+            first = lax.optimization_barrier((*first, *ready))[:2]
+        terms = other_terms(scal, act_t, grad, first, shard)
         if not last:
-            third = max(far - 1, 1)
+            third = max(n // 2 - 1, 1)
             terms[0][third] = after(terms[0][third], sib, moments[1])
         parts = ring.scatter_sum(terms)
         if not last:

time: 190 us -> 181 us (0.953); the launches traced: 190 us -> 178 us
  waiting for transfers between devices: 79.5 us -> 71.8 us
  starting transfers between devices: 68.5 us -> 61.9 us
  Pallas kernels: 35.3 us -> 41.7 us
  other arithmetic: 3.42 us -> 0.09 us
    pallas_call x10 -> x18, Pallas kernels: 13.5 us -> 36.1 us  [whole_call(): pl.pallas_call(kernel, in_specs=[SCALARS] * len(scalars) + [pl.BlockSpec(...]
    pallas_call x4 -> x0, Pallas kernels: 16.2 us -> none  [the longest x2 8.54 us: forward(): pl.pallas_call(partial(forward_kernel, per_col, scaling, n), in_specs=[SC...]
    ppermute x56, starting transfers between devices: 65 us -> 58.4 us  [move(): return lax.ppermute(x, 'fsdp', self.to_left if direction else self.to_right)]
    ppermute x56, waiting for transfers between devices: 64.9 us -> 59.6 us  [move(): return lax.ppermute(x, 'fsdp', self.to_left if direction else self.to_right)]
    mul x1 -> x0, other arithmetic: 2.13 us -> none  [mean(): 0.5 * (own + lax.ppermute(own.astype(bf16), 'rep', shift).astype(f32))]
  transfers between devices with their start and end apart: 66 -> 66, of which waited for: 36 -> 40; matrix products, arithmetic and copies ran while one was open for 0% -> 0% of each run, Pallas kernels for 11% -> 18%
where the time goes in v1:
time: 181 us; the launch traced here: 178 us
  waiting for transfers between devices  71.8 us (40%)
  starting transfers between devices  61.9 us (34%)
  Pallas kernels  41.7 us (23%)
  between operations  1.95 us (1%)
    ppermute x56, waiting for transfers between devices, move(): return lax.ppermute(x, 'fsdp', self.to_left if direction else self.to_right)  59.6 us
    ppermute x56, starting transfers between devices, move(): return lax.ppermute(x, 'fsdp', self.to_left if direction else self.to_right)  58.4 us
    pallas_call x18, Pallas kernels, whole_call(): pl.pallas_call(kernel, in_specs=[SCALARS] * len(scalars) + [pl.BlockSpec(...  36.1 us
    ppermute x1, waiting for transfers between devices, partner_of(): moved = lambda x, last, shift=shift: lax.ppermute(x, 'rep', shift)  8.96 us
  transfers between devices with their start and end apart: 66, of which 40 were waited for; matrix products, arithmetic and copies ran while one was open for 0% of the time, Pallas kernels for 18%

profile of v1, /device:TPU:0, one launch (start us, length us, event | category | flops | bytes accessed | tf_op | source)
XLA Modules:
  0.0 177.8 jit_solution(13936499872041423974)
XLA Ops:
  5.7 3.0 %collective-permute-start.11 = (bf16[10,5,16,128]{3,2,1,0:T(8,128)(2,1)S(1)}, bf16[10,5,16,128]{3,2,1,0:T(8,128)(2,1)S(1)}, u32[]{:S(2)}, u32[]{:S(2)}) collective-permute-start(bf16[10,5,16,128]{3,2,1,0:T(8,128)(2,1)S(1)} %get-tuple-element.114.refs_7_), channel_id=1, source_target_pairs={{4,0},{5,1},{8,4},{9,5},{12,8},{13,9},{14,12},{15,13},{10,14},{11,... | collective-permute-start | bytes 614408 | tf_op jit(solution)/shard_map/ppermute | solution.py:88
  12.5 2.2 %collective-permute-done.11.refs_8_ = bf16[10,5,16,128]{3,2,1,0:T(8,128)(2,1)S(1)} collective-permute-done((bf16[10,5,16,128]{3,2,1,0:T(8,128)(2,1)S(1)}, bf16[10,5,16,128]{3,2,1,0:T(8,128)(2,1)S(1)}, u32[]{:S(2)}, u32[]{:S(2)}) %collective-permute-start.11) | collective-permute-done | bytes 204832 | tf_op jit(solution)/shard_map/ppermute | solution.py:88
  14.7 2.0 %collective-permute-start.12 = (bf16[10,5,16,128]{3,2,1,0:T(8,128)(2,1)S(1)}, bf16[10,5,16,128]{3,2,1,0:T(8,128)(2,1)S(1)}, u32[]{:S(2)}, u32[]{:S(2)}) collective-permute-start(bf16[10,5,16,128]{3,2,1,0:T(8,128)(2,1)S(1)} %collective-permute-done.11.refs_8_), channel_id=1, source_target_pairs={{4,0},{5,1},{8,4},{9,5},{12,8},{13,9},{14,12},{15,13},{10,14},{11,... | collective-permute-start | bytes 614408 | tf_op jit(solution)/shard_map/ppermute | solution.py:88
  18.7 2.4 %collective-permute-done.3.refs_13_ = bf16[10,5,16,128]{3,2,1,0:T(8,128)(2,1)S(1)} collective-permute-done((bf16[10,5,16,128]{3,2,1,0:T(8,128)(2,1)S(1)}, bf16[10,5,16,128]{3,2,1,0:T(8,128)(2,1)S(1)}, u32[]{:S(2)}, u32[]{:S(2)}) %collective-permute-start.3) | collective-permute-done | bytes 204832 | tf_op jit(solution)/shard_map/ppermute | solution.py:88
  23.4 2.0 %collective-permute-start.13 = (bf16[10,5,16,128]{3,2,1,0:T(8,128)(2,1)S(1)}, bf16[10,5,16,128]{3,2,1,0:T(8,128)(2,1)S(1)}, u32[]{:S(2)}, u32[]{:S(2)}) collective-permute-start(bf16[10,5,16,128]{3,2,1,0:T(8,128)(2,1)S(1)} %collective-permute-done.12.refs_9_), channel_id=1, source_target_pairs={{4,0},{5,1},{8,4},{9,5},{12,8},{13,9},{14,12},{15,13},{10,14},{11,... | collective-permute-start | bytes 614408 | tf_op jit(solution)/shard_map/ppermute | solution.py:88
  31.1 2.4 %collective-permute-done.13.refs_10_ = bf16[10,5,16,128]{3,2,1,0:T(8,128)(2,1)S(1)} collective-permute-done((bf16[10,5,16,128]{3,2,1,0:T(8,128)(2,1)S(1)}, bf16[10,5,16,128]{3,2,1,0:T(8,128)(2,1)S(1)}, u32[]{:S(2)}, u32[]{:S(2)}) %collective-permute-start.13) | collective-permute-done | bytes 204832 | tf_op jit(solution)/shard_map/ppermute | solution.py:88
  35.5 2.4 %collective-permute-done.7.refs_3_ = bf16[10,5,16,128]{3,2,1,0:T(8,128)(2,1)S(1)} collective-permute-done((bf16[10,5,16,128]{3,2,1,0:T(8,128)(2,1)S(1)}, bf16[10,5,16,128]{3,2,1,0:T(8,128)(2,1)S(1)}, u32[]{:S(2)}, u32[]{:S(2)}) %collective-permute-start.7) | collective-permute-done | bytes 204832 | tf_op jit(solution)/shard_map/ppermute | solution.py:88
  39.6 4.1 %forward.2.part = f32[2,176,2560]{2,1,0:T(8,128)S(1)} custom-call(s32[109]{0:T(128)S(1)} %pad_add_fusion.scal, bf16[20,128,384]{2,1,0:T(8,128)(2,1)S(1)} %turn.2.act_t, bf16[2,176,2560]{2,1,0:T(8,128)(2,1)S(1)} %pick.5.kept, bf16[3,176,2560]{2,1,0:T(8,128)(2,1)S(1)} %collective-permute-done.4.sib, bf16[10,5,16,128]{3,2,1,0:T(8,128)(2,1)S(1)} %get-tuple-element.121.refs_0_, ...), custom_call_target="tpu_custom_call" | custom-call | flops 1153433600 | bytes 16777216 | tf_op jit(solution)/shard_map/forward/pallas_call | solution.py:135
  47.7 2.0 %backward.2 = (bf16[10,5,16,128]{3,2,1,0:T(8,128)(2,1)S(1)}, bf16[10,5,16,128]{3,2,1,0:T(8,128)(2,1)S(1)}, bf16[20,384,128]{2,1,0:T(8,128)(2,1)S(1)}) custom-call(s32[109]{0:T(128)S(1)} %pad_add_fusion.scal, bf16[20,128,384]{2,1,0:T(8,128)(2,1)S(1)} %turn.2.act_t, f32[2,176,2560]{2,1,0:T(8,128)S(1)} %get-tuple-element.131.pre, ...), custom_call_target="tpu_custom_call" | custom-call | flops 144179200 | bytes 16777216 | tf_op jit(solution)/shard_map/backward/pallas_call | solution.py:135
  51.8 3.3 %terms.2 = (bf16[10,5,16,128]{3,2,1,0:T(8,128)(2,1)S(1)}, bf16[10,5,16,128]{3,2,1,0:T(8,128)(2,1)S(1)}, bf16[10,5,16,128]{3,2,1,0:T(8,128)(2,1)S(1)}, bf16[10,5,...) custom-call(s32[109]{0:T(128)S(1)} %pad_add_fusion.scal, ...), custom_call_target="tpu_custom_call" | custom-call | flops 1258291200 | bytes 16777216 | tf_op jit(solution)/shard_map/terms/pallas_call | solution.py:135
  59.8 3.3 %collective-permute-done.25.a = bf16[10,5,16,128]{3,2,1,0:T(8,128)(2,1)S(1)} collective-permute-done((bf16[10,5,16,128]{3,2,1,0:T(8,128)(2,1)S(1)}, bf16[10,5,16,128]{3,2,1,0:T(8,128)(2,1)S(1)}, u32[]{:S(2)}, u32[]{:S(2)}) %collective-permute-start.25) | collective-permute-done | bytes 204832 | tf_op jit(solution)/shard_map/ppermute | solution.py:88
  80.7 2.1 %collective-permute-done.30.refs_4_ = bf16[10,5,16,128]{3,2,1,0:T(8,128)(2,1)S(1)} collective-permute-done((bf16[10,5,16,128]{3,2,1,0:T(8,128)(2,1)S(1)}, bf16[10,5,16,128]{3,2,1,0:T(8,128)(2,1)S(1)}, u32[]{:S(2)}, u32[]{:S(2)}) %collective-permute-start.30) | collective-permute-done | bytes 204832 | tf_op jit(solution)/shard_map/ppermute | solution.py:88
  87.6 10.5 %conditional.2 = (bf16[20,5,16,128]{3,2,1,0:T(8,128)(2,1)}) conditional(s32[]{:T(128)} %convert_element_type.12, () %tuple.82, bf16[20,5,16,128]{3,2,1,0:T(8,128)(2,1)} %get-tuple-element.160), branch_computations={%region_0.1_spmd, %region_1.2_spmd} | conditional | bytes 1638448 | solution.py:741
  89.1 9.0 %collective-permute-done = bf16[20,5,16,128]{3,2,1,0:T(8,128)(2,1)} collective-permute-done((bf16[20,5,16,128]{3,2,1,0:T(8,128)(2,1)}, bf16[20,5,16,128]{3,2,1,0:T(8,128)(2,1)}, u32[]{:S(2)}, u32[]{:S(2)}) %collective-permute-start) | collective-permute-done | bytes 409632 | tf_op jit(solution)/shard_map/cond/branch_1_fun/ppermute | solution.py:739
  105.3 2.3 %collective-permute-done.39.refs_6_ = bf16[10,5,16,128]{3,2,1,0:T(8,128)(2,1)S(1)} collective-permute-done((bf16[10,5,16,128]{3,2,1,0:T(8,128)(2,1)S(1)}, bf16[10,5,16,128]{3,2,1,0:T(8,128)(2,1)S(1)}, u32[]{:S(2)}, u32[]{:S(2)}) %collective-permute-start.39) | collective-permute-done | bytes 204832 | tf_op jit(solution)/shard_map/ppermute | solution.py:88
  109.6 2.4 %collective-permute-done.35.refs_13_ = bf16[10,5,16,128]{3,2,1,0:T(8,128)(2,1)S(1)} collective-permute-done((bf16[10,5,16,128]{3,2,1,0:T(8,128)(2,1)S(1)}, bf16[10,5,16,128]{3,2,1,0:T(8,128)(2,1)S(1)}, u32[]{:S(2)}, u32[]{:S(2)}) %collective-permute-start.35) | collective-permute-done | bytes 204832 | tf_op jit(solution)/shard_map/ppermute | solution.py:88
  122.8 3.1 %collective-permute-done.44.refs_10_ = bf16[10,5,16,128]{3,2,1,0:T(8,128)(2,1)S(1)} collective-permute-done((bf16[10,5,16,128]{3,2,1,0:T(8,128)(2,1)S(1)}, bf16[10,5,16,128]{3,2,1,0:T(8,128)(2,1)S(1)}, u32[]{:S(2)}, u32[]{:S(2)}) %collective-permute-start.44) | collective-permute-done | bytes 204832 | tf_op jit(solution)/shard_map/ppermute | solution.py:88
  129.2 4.1 %forward.3.part = f32[2,176,2560]{2,1,0:T(8,128)S(1)} custom-call(s32[109]{0:T(128)S(1)} %pad_add_fusion.scal, bf16[20,128,384]{2,1,0:T(8,128)(2,1)S(1)} %turn.3.act_t, bf16[2,176,2560]{2,1,0:T(8,128)(2,1)S(1)} %pick.7.kept, bf16[3,176,2560]{2,1,0:T(8,128)(2,1)S(1)} %collective-permute-done.20.sib, bf16[10,5,16,128]{3,2,1,0:T(8,128)(2,1)S(1)} %get-tuple-element.164.refs_0_, ...), custom_call_target="tpu_custom_call" | custom-call | flops 1153433600 | bytes 16777216 | tf_op jit(solution)/shard_map/forward/pallas_call | solution.py:135
  141.3 3.3 %terms.3 = (bf16[10,5,16,128]{3,2,1,0:T(8,128)(2,1)S(1)}, bf16[10,5,16,128]{3,2,1,0:T(8,128)(2,1)S(1)}, bf16[10,5,16,128]{3,2,1,0:T(8,128)(2,1)S(1)}, bf16[10,5,...) custom-call(s32[109]{0:T(128)S(1)} %pad_add_fusion.scal, ...), custom_call_target="tpu_custom_call" | custom-call | flops 1258291200 | bytes 16777216 | tf_op jit(solution)/shard_map/terms/pallas_call | solution.py:135
  149.0 3.7 %collective-permute-done.56.a = bf16[10,5,16,128]{3,2,1,0:T(8,128)(2,1)S(1)} collective-permute-done((bf16[10,5,16,128]{3,2,1,0:T(8,128)(2,1)S(1)}, bf16[10,5,16,128]{3,2,1,0:T(8,128)(2,1)S(1)}, u32[]{:S(2)}, u32[]{:S(2)}) %collective-permute-start.56) | collective-permute-done | bytes 204832 | tf_op jit(solution)/shard_map/ppermute | solution.py:88
  155.0 3.4 %collective-permute-done.53.a = bf16[10,5,16,128]{3,2,1,0:T(8,128)(2,1)S(1)} collective-permute-done((bf16[10,5,16,128]{3,2,1,0:T(8,128)(2,1)S(1)}, bf16[10,5,16,128]{3,2,1,0:T(8,128)(2,1)S(1)}, u32[]{:S(2)}, u32[]{:S(2)}) %collective-permute-start.53) | collective-permute-done | bytes 204832 | tf_op jit(solution)/shard_map/ppermute | solution.py:88
  163.7 3.4 %collective-permute-done.54.a = bf16[10,5,16,128]{3,2,1,0:T(8,128)(2,1)S(1)} collective-permute-done((bf16[10,5,16,128]{3,2,1,0:T(8,128)(2,1)S(1)}, bf16[10,5,16,128]{3,2,1,0:T(8,128)(2,1)S(1)}, u32[]{:S(2)}, u32[]{:S(2)}) %collective-permute-start.54) | collective-permute-done | bytes 204832 | tf_op jit(solution)/shard_map/ppermute | solution.py:88
  169.3 2.0 %collective-permute-done.58.refs_2_ = bf16[10,5,16,128]{3,2,1,0:T(8,128)(2,1)S(1)} collective-permute-done((bf16[10,5,16,128]{3,2,1,0:T(8,128)(2,1)S(1)}, bf16[10,5,16,128]{3,2,1,0:T(8,128)(2,1)S(1)}, u32[]{:S(2)}, u32[]{:S(2)}) %collective-permute-start.58) | collective-permute-done | bytes 204832 | tf_op jit(solution)/shard_map/ppermute | solution.py:88
  171.5 2.6 %collective-permute-done.55.refs_1_ = bf16[10,5,16,128]{3,2,1,0:T(8,128)(2,1)S(1)} collective-permute-done((bf16[10,5,16,128]{3,2,1,0:T(8,128)(2,1)S(1)}, bf16[10,5,16,128]{3,2,1,0:T(8,128)(2,1)S(1)}, u32[]{:S(2)}, u32[]{:S(2)}) %collective-permute-start.55) | collective-permute-done | bytes 204832 | tf_op jit(solution)/shard_map/ppermute | solution.py:88
  (170 shorter events, 105.5 us)
Async XLA Ops:
  5.5 19.9 %collective-permute-start.4 = (bf16[3,176,2560]{2,1,0:T(8,128)(2,1)S(1)}, bf16[3,176,2560]{2,1,0:T(8,128)(2,1)S(1)}, u32[]{:S(2)}, u32[]{:S(2)}) collective-permute-start(bf16[3,176,2560]{2,1,0:T(8,128)(2,1)S(1)} %pick.4.own), channel_id=1, source_target_pairs={{0,1},{1,0},{2,3},{3,2},{4,5},{5,4},{6,7},{7,6},{8,9},{9,8},{10,11... | collective-permute-start | bytes 8110088 | tf_op jit(solution)/shard_map/ppermute | solution.py:74
  5.7 9.0 %collective-permute-start.11 = (bf16[10,5,16,128]{3,2,1,0:T(8,128)(2,1)S(1)}, bf16[10,5,16,128]{3,2,1,0:T(8,128)(2,1)S(1)}, u32[]{:S(2)}, u32[]{:S(2)}) collective-permute-start(bf16[10,5,16,128]{3,2,1,0:T(8,128)(2,1)S(1)} %get-tuple-element.114.refs_7_), channel_id=1, source_target_pairs={{4,0},{5,1},{8,4},{9,5},{12,8},{13,9},{14,12},{15,13},{10,14},{11,... | collective-permute-start | bytes 614408 | tf_op jit(solution)/shard_map/ppermute | solution.py:88
  8.8 12.2 %collective-permute-start.3 = (bf16[10,5,16,128]{3,2,1,0:T(8,128)(2,1)S(1)}, bf16[10,5,16,128]{3,2,1,0:T(8,128)(2,1)S(1)}, u32[]{:S(2)}, u32[]{:S(2)}) collective-permute-start(bf16[10,5,16,128]{3,2,1,0:T(8,128)(2,1)S(1)} %get-tuple-element.114.refs_7_), channel_id=1, source_target_pairs={{0,4},{1,5},{4,8},{5,9},{8,12},{9,13},{12,14},{13,15},{14,10},{15,... | collective-permute-start | bytes 614408 | tf_op jit(solution)/shard_map/ppermute | solution.py:88
  10.8 10.3 %collective-permute-start.5 = (bf16[10,5,16,128]{3,2,1,0:T(8,128)(2,1)S(1)}, bf16[10,5,16,128]{3,2,1,0:T(8,128)(2,1)S(1)}, u32[]{:S(2)}, u32[]{:S(2)}) collective-permute-start(bf16[10,5,16,128]{3,2,1,0:T(8,128)(2,1)S(1)} %get-tuple-element.121.refs_0_), channel_id=1, source_target_pairs={{4,0},{5,1},{8,4},{9,5},{12,8},{13,9},{14,12},{15,13},{10,14},{11,... | collective-permute-start | bytes 614408 | tf_op jit(solution)/shard_map/ppermute | solution.py:88
  14.7 8.8 %collective-permute-start.12 = (bf16[10,5,16,128]{3,2,1,0:T(8,128)(2,1)S(1)}, bf16[10,5,16,128]{3,2,1,0:T(8,128)(2,1)S(1)}, u32[]{:S(2)}, u32[]{:S(2)}) collective-permute-start(bf16[10,5,16,128]{3,2,1,0:T(8,128)(2,1)S(1)} %collective-permute-done.11.refs_8_), channel_id=1, source_target_pairs={{4,0},{5,1},{8,4},{9,5},{12,8},{13,9},{14,12},{15,13},{10,14},{11,... | collective-permute-start | bytes 614408 | tf_op jit(solution)/shard_map/ppermute | solution.py:88
  16.7 10.5 %collective-permute-start.9 = (bf16[10,5,16,128]{3,2,1,0:T(8,128)(2,1)S(1)}, bf16[10,5,16,128]{3,2,1,0:T(8,128)(2,1)S(1)}, u32[]{:S(2)}, u32[]{:S(2)}) collective-permute-start(bf16[10,5,16,128]{3,2,1,0:T(8,128)(2,1)S(1)} %collective-permute-done.8.refs_6_), channel_id=1, source_target_pairs={{0,4},{1,5},{4,8},{5,9},{8,12},{9,13},{12,14},{13,15},{14,10},{15,... | collective-permute-start | bytes 614408 | tf_op jit(solution)/shard_map/ppermute | solution.py:88
  23.4 10.1 %collective-permute-start.13 = (bf16[10,5,16,128]{3,2,1,0:T(8,128)(2,1)S(1)}, bf16[10,5,16,128]{3,2,1,0:T(8,128)(2,1)S(1)}, u32[]{:S(2)}, u32[]{:S(2)}) collective-permute-start(bf16[10,5,16,128]{3,2,1,0:T(8,128)(2,1)S(1)} %collective-permute-done.12.refs_9_), channel_id=1, source_target_pairs={{4,0},{5,1},{8,4},{9,5},{12,8},{13,9},{14,12},{15,13},{10,14},{11,... | collective-permute-start | bytes 614408 | tf_op jit(solution)/shard_map/ppermute | solution.py:88
  29.1 8.8 %collective-permute-start.7 = (bf16[10,5,16,128]{3,2,1,0:T(8,128)(2,1)S(1)}, bf16[10,5,16,128]{3,2,1,0:T(8,128)(2,1)S(1)}, u32[]{:S(2)}, u32[]{:S(2)}) collective-permute-start(bf16[10,5,16,128]{3,2,1,0:T(8,128)(2,1)S(1)} %collective-permute-done.6.refs_2_), channel_id=1, source_target_pairs={{4,0},{5,1},{8,4},{9,5},{12,8},{13,9},{14,12},{15,13},{10,14},{11,... | collective-permute-start | bytes 614408 | tf_op jit(solution)/shard_map/ppermute | solution.py:88
  30.7 8.9 %collective-permute-start.15 = (bf16[10,5,16,128]{3,2,1,0:T(8,128)(2,1)S(1)}, bf16[10,5,16,128]{3,2,1,0:T(8,128)(2,1)S(1)}, u32[]{:S(2)}, u32[]{:S(2)}) collective-permute-start(bf16[10,5,16,128]{3,2,1,0:T(8,128)(2,1)S(1)} %collective-permute-done.14.refs_12_), channel_id=1, source_target_pairs={{0,4},{1,5},{4,8},{5,9},{8,12},{9,13},{12,14},{13,15},{14,10},{15,... | collective-permute-start | bytes 614408 | tf_op jit(solution)/shard_map/ppermute | solution.py:88
  33.5 10.2 %collective-permute-start.17 = (bf16[10,5,16,128]{3,2,1,0:T(8,128)(2,1)S(1)}, bf16[10,5,16,128]{3,2,1,0:T(8,128)(2,1)S(1)}, u32[]{:S(2)}, u32[]{:S(2)}) collective-permute-start(bf16[10,5,16,128]{3,2,1,0:T(8,128)(2,1)S(1)} %collective-permute-done.13.refs_10_), channel_id=1, source_target_pairs={{4,0},{5,1},{8,4},{9,5},{12,8},{13,9},{14,12},{15,13},{10,14},{11,... | collective-permute-start | bytes 614408 | tf_op jit(solution)/shard_map/ppermute | solution.py:88
  47.2 12.2 %collective-permute-start.20 = (bf16[3,176,2560]{2,1,0:T(8,128)(2,1)S(1)}, bf16[3,176,2560]{2,1,0:T(8,128)(2,1)S(1)}, u32[]{:S(2)}, u32[]{:S(2)}) collective-permute-start(bf16[3,176,2560]{2,1,0:T(8,128)(2,1)S(1)} %pick.6.own), channel_id=1, source_target_pairs={{0,1},{1,0},{2,3},{3,2},{4,5},{5,4},{6,7},{7,6},{8,9},{9,8},{10,11... | collective-permute-start | bytes 8110088 | tf_op jit(solution)/shard_map/ppermute | solution.py:74
  47.7 10.0 %collective-permute-start.21 = (f32[20,5,8,128]{3,2,1,0:T(8,128)S(1)}, f32[20,5,8,128]{3,2,1,0:T(8,128)S(1)}, u32[]{:S(2)}, u32[]{:S(2)}) collective-permute-start(f32[20,5,8,128]{3,2,1,0:T(8,128)S(1)} %get-tuple-element.142), channel_id=1, source_target_pairs={{0,1},{1,0},{2,3},{3,2},{4,5},{5,4},{6,7},{7,6},{8,9},{9,8},{10,11... | collective-permute-start | bytes 1228808 | tf_op jit(solution)/shard_map/ppermute | solution.py:74
  57.6 9.9 %collective-permute-start.32 = (bf16[10,5,16,128]{3,2,1,0:T(8,128)(2,1)S(1)}, bf16[10,5,16,128]{3,2,1,0:T(8,128)(2,1)S(1)}, u32[]{:S(2)}, u32[]{:S(2)}) collective-permute-start(bf16[10,5,16,128]{3,2,1,0:T(8,128)(2,1)S(1)} %add.60), channel_id=1, source_target_pairs={{4,0},{5,1},{8,4},{9,5},{12,8},{13,9},{14,12},{15,13},{10,14},{11,... | collective-permute-start | bytes 614408 | tf_op jit(solution)/shard_map/ppermute | solution.py:88
  59.5 10.2 %collective-permute-start.22 = (bf16[10,5,16,128]{3,2,1,0:T(8,128)(2,1)S(1)}, bf16[10,5,16,128]{3,2,1,0:T(8,128)(2,1)S(1)}, u32[]{:S(2)}, u32[]{:S(2)}) collective-permute-start(bf16[10,5,16,128]{3,2,1,0:T(8,128)(2,1)S(1)} %add.53), channel_id=1, source_target_pairs={{0,4},{1,5},{4,8},{5,9},{8,12},{9,13},{12,14},{13,15},{14,10},{15,... | collective-permute-start | bytes 614408 | tf_op jit(solution)/shard_map/ppermute | solution.py:88
  87.6 10.5 %collective-permute-start = (bf16[20,5,16,128]{3,2,1,0:T(8,128)(2,1)}, bf16[20,5,16,128]{3,2,1,0:T(8,128)(2,1)}, u32[]{:S(2)}, u32[]{:S(2)}) collective-permute-start(bf16[20,5,16,128]{3,2,1,0:T(8,128)(2,1)} %param.1), channel_id=1, source_target_pairs={{0,16},{16,0},{1,17},{17,1},{2,18},{18,2},{3,19},{19,3},{4,20},{20... | collective-permute-start | bytes 1228808 | tf_op jit(solution)/shard_map/cond/branch_1_fun/ppermute | solution.py:739
  101.6 10.4 %collective-permute-start.35 = (bf16[10,5,16,128]{3,2,1,0:T(8,128)(2,1)S(1)}, bf16[10,5,16,128]{3,2,1,0:T(8,128)(2,1)S(1)}, u32[]{:S(2)}, u32[]{:S(2)}) collective-permute-start(bf16[10,5,16,128]{3,2,1,0:T(8,128)(2,1)S(1)} %get-tuple-element.162.refs_7_), channel_id=1, source_target_pairs={{0,4},{1,5},{4,8},{5,9},{8,12},{9,13},{12,14},{13,15},{14,10},{15,... | collective-permute-start | bytes 614408 | tf_op jit(solution)/shard_map/ppermute | solution.py:88
  102.3 10.4 %collective-permute-start.36 = (bf16[10,5,16,128]{3,2,1,0:T(8,128)(2,1)S(1)}, bf16[10,5,16,128]{3,2,1,0:T(8,128)(2,1)S(1)}, u32[]{:S(2)}, u32[]{:S(2)}) collective-permute-start(bf16[10,5,16,128]{3,2,1,0:T(8,128)(2,1)S(1)} %get-tuple-element.164.refs_0_), channel_id=1, source_target_pairs={{4,0},{5,1},{8,4},{9,5},{12,8},{13,9},{14,12},{15,13},{10,14},{11,... | collective-permute-start | bytes 614408 | tf_op jit(solution)/shard_map/ppermute | solution.py:88
  107.6 8.8 %collective-permute-start.40 = (bf16[10,5,16,128]{3,2,1,0:T(8,128)(2,1)S(1)}, bf16[10,5,16,128]{3,2,1,0:T(8,128)(2,1)S(1)}, u32[]{:S(2)}, u32[]{:S(2)}) collective-permute-start(bf16[10,5,16,128]{3,2,1,0:T(8,128)(2,1)S(1)} %collective-permute-done.39.refs_6_), channel_id=1, source_target_pairs={{0,4},{1,5},{4,8},{5,9},{8,12},{9,13},{12,14},{13,15},{14,10},{15,... | collective-permute-start | bytes 614408 | tf_op jit(solution)/shard_map/ppermute | solution.py:88
  112.0 8.8 %collective-permute-start.45 = (bf16[10,5,16,128]{3,2,1,0:T(8,128)(2,1)S(1)}, bf16[10,5,16,128]{3,2,1,0:T(8,128)(2,1)S(1)}, u32[]{:S(2)}, u32[]{:S(2)}) collective-permute-start(bf16[10,5,16,128]{3,2,1,0:T(8,128)(2,1)S(1)} %collective-permute-done.35.refs_13_), channel_id=1, source_target_pairs={{0,4},{1,5},{4,8},{5,9},{8,12},{9,13},{12,14},{13,15},{14,10},{15,... | collective-permute-start | bytes 614408 | tf_op jit(solution)/shard_map/ppermute | solution.py:88
  117.1 8.8 %collective-permute-start.44 = (bf16[10,5,16,128]{3,2,1,0:T(8,128)(2,1)S(1)}, bf16[10,5,16,128]{3,2,1,0:T(8,128)(2,1)S(1)}, u32[]{:S(2)}, u32[]{:S(2)}) collective-permute-start(bf16[10,5,16,128]{3,2,1,0:T(8,128)(2,1)S(1)} %collective-permute-done.43.refs_9_), channel_id=1, source_target_pairs={{4,0},{5,1},{8,4},{9,5},{12,8},{13,9},{14,12},{15,13},{10,14},{11,... | collective-permute-start | bytes 614408 | tf_op jit(solution)/shard_map/ppermute | solution.py:88
  118.4 8.8 %collective-permute-start.41 = (bf16[10,5,16,128]{3,2,1,0:T(8,128)(2,1)S(1)}, bf16[10,5,16,128]{3,2,1,0:T(8,128)(2,1)S(1)}, u32[]{:S(2)}, u32[]{:S(2)}) collective-permute-start(bf16[10,5,16,128]{3,2,1,0:T(8,128)(2,1)S(1)} %collective-permute-done.40.refs_5_), channel_id=1, source_target_pairs={{0,4},{1,5},{4,8},{5,9},{8,12},{9,13},{12,14},{13,15},{14,10},{15,... | collective-permute-start | bytes 614408 | tf_op jit(solution)/shard_map/ppermute | solution.py:88
  146.8 11.5 %collective-permute-start.53 = (bf16[10,5,16,128]{3,2,1,0:T(8,128)(2,1)S(1)}, bf16[10,5,16,128]{3,2,1,0:T(8,128)(2,1)S(1)}, u32[]{:S(2)}, u32[]{:S(2)}) collective-permute-start(bf16[10,5,16,128]{3,2,1,0:T(8,128)(2,1)S(1)} %add.63), channel_id=1, source_target_pairs={{0,4},{1,5},{4,8},{5,9},{8,12},{9,13},{12,14},{13,15},{14,10},{15,... | collective-permute-start | bytes 614408 | tf_op jit(solution)/shard_map/ppermute | solution.py:88
  148.0 11.2 %collective-permute-start.63 = (bf16[10,5,16,128]{3,2,1,0:T(8,128)(2,1)S(1)}, bf16[10,5,16,128]{3,2,1,0:T(8,128)(2,1)S(1)}, u32[]{:S(2)}, u32[]{:S(2)}) collective-permute-start(bf16[10,5,16,128]{3,2,1,0:T(8,128)(2,1)S(1)} %add.70), channel_id=1, source_target_pairs={{4,0},{5,1},{8,4},{9,5},{12,8},{13,9},{14,12},{15,13},{10,14},{11,... | collective-permute-start | bytes 614408 | tf_op jit(solution)/shard_map/ppermute | solution.py:88
  161.5 9.8 %collective-permute-start.58 = (bf16[10,5,16,128]{3,2,1,0:T(8,128)(2,1)S(1)}, bf16[10,5,16,128]{3,2,1,0:T(8,128)(2,1)S(1)}, u32[]{:S(2)}, u32[]{:S(2)}) collective-permute-start(bf16[10,5,16,128]{3,2,1,0:T(8,128)(2,1)S(1)} %add.67), channel_id=1, source_target_pairs={{4,0},{5,1},{8,4},{9,5},{12,8},{13,9},{14,12},{15,13},{10,14},{11,... | collective-permute-start | bytes 614408 | tf_op jit(solution)/shard_map/ppermute | solution.py:88
  (49 other events, 391.0 us)

commit v2 on v1

--- a/solution.py
+++ b/solution.py
@@ -208,6 +208,13 @@
     moments_out, weights_out, low = near[:2], near[2:4], near[4]
     half_cols = low.shape[0] // 2
 
+    cuts = [pl.ds(h * half_cols, half_cols) for h in range(2)]
+    copies = [
+        pltpu.make_async_copy(near[i].at[cut], far[i].at[cut], sems.at[i, h])
+        for h, cut in enumerate(cuts)
+        for i in range(5)
+    ]
+
     def body(core):
         for h in range(2):
 
@@ -222,11 +229,10 @@
                 low[at] = halves_of(*news, core).astype(bf16)
 
             columns_loop(half_cols, column)
+            for copy in copies[5 * h : 5 * h + 5]:
+                copy.start()
 
     by_core(body)
-    copies = [pltpu.make_async_copy(near[i], far[i], sems.at[i]) for i in range(5)]
-    for copy in copies:
-        copy.start()
     for copy in copies:
         copy.wait()
 
@@ -242,7 +248,7 @@
         out_specs=[pl.BlockSpec(memory_space=pl.ANY)] * 5,
         out_shape=[pltpu.HBM(x.shape, x.dtype) for x in outs],
         scratch_shapes=[pltpu.VMEM(x.shape, x.dtype) for x in outs]
-        + [pltpu.SemaphoreType.DMA((5,))],
+        + [pltpu.SemaphoreType.DMA((5, 2))],
         compiler_params=PARAMS,
         cost_estimate=pl.CostEstimate(
             flops=rows.size * 20, bytes_accessed=rows.size * 60, transcendentals=0
@@ -830,7 +836,7 @@
             given = state["later"]
             sib = ring.swap(after(given, other))
         if s == 0:
-            moments = [moments[0], ring.swap(after(moments[1], other))]
+            moments = [moments[0], ring.swap(after(moments[1], sib))]
         if last:
             moments = [moments[0], ring.swap(after(moments[1], other))]
             weights = [weights[0], ring.swap(after(weights[1], other))]
@@ -840,7 +846,7 @@
         terms = other_terms(scal, act_t, grad, first, shard)
         if not last:
             third = max(n // 2 - 1, 1)
-            terms[0][third] = after(terms[0][third], sib, moments[1])
+            terms[0][third] = after(terms[0][third], sib)
         parts = ring.scatter_sum(terms)
         if not last:
             moments, weights, low = update(parts, moments, weights, scaling, shard)

time: 181 us -> 180 us (level)
  transfers between devices with their start and end apart: 66 -> 66, of which waited for: 40 -> 35; matrix products, arithmetic and copies ran while one was open for 0% -> 0% of each run, Pallas kernels for 18% -> 18%
where the time goes in v2:
time: 180 us; the launch traced here: 176 us
  waiting for transfers between devices  70 us (39%)
  starting transfers between devices  62.5 us (35%)
  Pallas kernels  41.5 us (23%)
  between operations  1.94 us (1%)
    ppermute x56, starting transfers between devices, move(): return lax.ppermute(x, 'fsdp', self.to_left if direction else self.to_right)  59.1 us
    ppermute x56, waiting for transfers between devices, move(): return lax.ppermute(x, 'fsdp', self.to_left if direction else self.to_right)  58 us
    pallas_call x18, Pallas kernels, whole_call(): pl.pallas_call(kernel, in_specs=[SCALARS] * len(scalars) + [pl.BlockSpec(...  36.1 us
    ppermute x1, waiting for transfers between devices, partner_of(): moved = lambda x, last, shift=shift: lax.ppermute(x, 'rep', shift)  8.73 us
  transfers between devices with their start and end apart: 66, of which 35 were waited for; matrix products, arithmetic and copies ran while one was open for 0% of the time, Pallas kernels for 18%

profile of v2, /device:TPU:0, one launch (start us, length us, event | category | flops | bytes accessed | tf_op | source)
XLA Modules:
  0.0 176.3 jit_solution(5532935826532477542)
XLA Ops:
  5.7 3.0 %collective-permute-start.11 = (bf16[10,5,16,128]{3,2,1,0:T(8,128)(2,1)S(1)}, bf16[10,5,16,128]{3,2,1,0:T(8,128)(2,1)S(1)}, u32[]{:S(2)}, u32[]{:S(2)}) collective-permute-start(bf16[10,5,16,128]{3,2,1,0:T(8,128)(2,1)S(1)} %get-tuple-element.114.refs_7_), channel_id=1, source_target_pairs={{4,0},{5,1},{8,4},{9,5},{12,8},{13,9},{14,12},{15,13},{10,14},{11,... | collective-permute-start | bytes 614408 | tf_op jit(solution)/shard_map/ppermute | solution.py:88
  12.5 2.2 %collective-permute-done.11.refs_8_ = bf16[10,5,16,128]{3,2,1,0:T(8,128)(2,1)S(1)} collective-permute-done((bf16[10,5,16,128]{3,2,1,0:T(8,128)(2,1)S(1)}, bf16[10,5,16,128]{3,2,1,0:T(8,128)(2,1)S(1)}, u32[]{:S(2)}, u32[]{:S(2)}) %collective-permute-start.11) | collective-permute-done | bytes 204832 | tf_op jit(solution)/shard_map/ppermute | solution.py:88
  18.7 2.4 %collective-permute-done.3.refs_13_ = bf16[10,5,16,128]{3,2,1,0:T(8,128)(2,1)S(1)} collective-permute-done((bf16[10,5,16,128]{3,2,1,0:T(8,128)(2,1)S(1)}, bf16[10,5,16,128]{3,2,1,0:T(8,128)(2,1)S(1)}, u32[]{:S(2)}, u32[]{:S(2)}) %collective-permute-start.3) | collective-permute-done | bytes 204832 | tf_op jit(solution)/shard_map/ppermute | solution.py:88
  23.4 2.0 %collective-permute-start.13 = (bf16[10,5,16,128]{3,2,1,0:T(8,128)(2,1)S(1)}, bf16[10,5,16,128]{3,2,1,0:T(8,128)(2,1)S(1)}, u32[]{:S(2)}, u32[]{:S(2)}) collective-permute-start(bf16[10,5,16,128]{3,2,1,0:T(8,128)(2,1)S(1)} %collective-permute-done.12.refs_9_), channel_id=1, source_target_pairs={{4,0},{5,1},{8,4},{9,5},{12,8},{13,9},{14,12},{15,13},{10,14},{11,... | collective-permute-start | bytes 614408 | tf_op jit(solution)/shard_map/ppermute | solution.py:88
  31.1 2.4 %collective-permute-done.13.refs_10_ = bf16[10,5,16,128]{3,2,1,0:T(8,128)(2,1)S(1)} collective-permute-done((bf16[10,5,16,128]{3,2,1,0:T(8,128)(2,1)S(1)}, bf16[10,5,16,128]{3,2,1,0:T(8,128)(2,1)S(1)}, u32[]{:S(2)}, u32[]{:S(2)}) %collective-permute-start.13) | collective-permute-done | bytes 204832 | tf_op jit(solution)/shard_map/ppermute | solution.py:88
  35.5 2.4 %collective-permute-done.7.refs_3_ = bf16[10,5,16,128]{3,2,1,0:T(8,128)(2,1)S(1)} collective-permute-done((bf16[10,5,16,128]{3,2,1,0:T(8,128)(2,1)S(1)}, bf16[10,5,16,128]{3,2,1,0:T(8,128)(2,1)S(1)}, u32[]{:S(2)}, u32[]{:S(2)}) %collective-permute-start.7) | collective-permute-done | bytes 204832 | tf_op jit(solution)/shard_map/ppermute | solution.py:88
  39.6 4.1 %forward.2.part = f32[2,176,2560]{2,1,0:T(8,128)S(1)} custom-call(s32[109]{0:T(128)S(1)} %pad_add_fusion.scal, bf16[20,128,384]{2,1,0:T(8,128)(2,1)S(1)} %turn.2.act_t, bf16[2,176,2560]{2,1,0:T(8,128)(2,1)S(1)} %pick.5.kept, bf16[3,176,2560]{2,1,0:T(8,128)(2,1)S(1)} %collective-permute-done.4.sib, bf16[10,5,16,128]{3,2,1,0:T(8,128)(2,1)S(1)} %get-tuple-element.121.refs_0_, ...), custom_call_target="tpu_custom_call" | custom-call | flops 1153433600 | bytes 16777216 | tf_op jit(solution)/shard_map/forward/pallas_call | solution.py:135
  51.7 3.3 %terms.2 = (bf16[10,5,16,128]{3,2,1,0:T(8,128)(2,1)S(1)}, bf16[10,5,16,128]{3,2,1,0:T(8,128)(2,1)S(1)}, bf16[10,5,16,128]{3,2,1,0:T(8,128)(2,1)S(1)}, bf16[10,5,...) custom-call(s32[109]{0:T(128)S(1)} %pad_add_fusion.scal, ...), custom_call_target="tpu_custom_call" | custom-call | flops 1258291200 | bytes 16777216 | tf_op jit(solution)/shard_map/terms/pallas_call | solution.py:135
  59.3 3.7 %collective-permute-done.24.a = bf16[10,5,16,128]{3,2,1,0:T(8,128)(2,1)S(1)} collective-permute-done((bf16[10,5,16,128]{3,2,1,0:T(8,128)(2,1)S(1)}, bf16[10,5,16,128]{3,2,1,0:T(8,128)(2,1)S(1)}, u32[]{:S(2)}, u32[]{:S(2)}) %collective-permute-start.24) | collective-permute-done | bytes 204832 | tf_op jit(solution)/shard_map/ppermute | solution.py:88
  65.3 2.1 %collective-permute-done.31.a = bf16[10,5,16,128]{3,2,1,0:T(8,128)(2,1)S(1)} collective-permute-done((bf16[10,5,16,128]{3,2,1,0:T(8,128)(2,1)S(1)}, bf16[10,5,16,128]{3,2,1,0:T(8,128)(2,1)S(1)}, u32[]{:S(2)}, u32[]{:S(2)}) %collective-permute-start.31) | collective-permute-done | bytes 204832 | tf_op jit(solution)/shard_map/ppermute | solution.py:88
  69.7 2.1 %collective-permute-done.25.a = bf16[10,5,16,128]{3,2,1,0:T(8,128)(2,1)S(1)} collective-permute-done((bf16[10,5,16,128]{3,2,1,0:T(8,128)(2,1)S(1)}, bf16[10,5,16,128]{3,2,1,0:T(8,128)(2,1)S(1)}, u32[]{:S(2)}, u32[]{:S(2)}) %collective-permute-start.25) | collective-permute-done | bytes 204832 | tf_op jit(solution)/shard_map/ppermute | solution.py:88
  74.1 2.1 %collective-permute-done.32.a = bf16[10,5,16,128]{3,2,1,0:T(8,128)(2,1)S(1)} collective-permute-done((bf16[10,5,16,128]{3,2,1,0:T(8,128)(2,1)S(1)}, bf16[10,5,16,128]{3,2,1,0:T(8,128)(2,1)S(1)}, u32[]{:S(2)}, u32[]{:S(2)}) %collective-permute-start.32) | collective-permute-done | bytes 204832 | tf_op jit(solution)/shard_map/ppermute | solution.py:88
  78.5 2.1 %collective-permute-done.26.refs_2_ = bf16[10,5,16,128]{3,2,1,0:T(8,128)(2,1)S(1)} collective-permute-done((bf16[10,5,16,128]{3,2,1,0:T(8,128)(2,1)S(1)}, bf16[10,5,16,128]{3,2,1,0:T(8,128)(2,1)S(1)}, u32[]{:S(2)}, u32[]{:S(2)}) %collective-permute-start.26) | collective-permute-done | bytes 204832 | tf_op jit(solution)/shard_map/ppermute | solution.py:88
  86.3 10.3 %conditional.2 = (bf16[20,5,16,128]{3,2,1,0:T(8,128)(2,1)}) conditional(s32[]{:T(128)} %convert_element_type.12, () %tuple.82, bf16[20,5,16,128]{3,2,1,0:T(8,128)(2,1)} %get-tuple-element.160), branch_computations={%region_0.1_spmd, %region_1.2_spmd} | conditional | bytes 1638448 | solution.py:747
  87.9 8.7 %collective-permute-done = bf16[20,5,16,128]{3,2,1,0:T(8,128)(2,1)} collective-permute-done((bf16[20,5,16,128]{3,2,1,0:T(8,128)(2,1)}, bf16[20,5,16,128]{3,2,1,0:T(8,128)(2,1)}, u32[]{:S(2)}, u32[]{:S(2)}) %collective-permute-start) | collective-permute-done | bytes 409632 | tf_op jit(solution)/shard_map/cond/branch_1_fun/ppermute | solution.py:745
  103.8 2.3 %collective-permute-done.39.refs_6_ = bf16[10,5,16,128]{3,2,1,0:T(8,128)(2,1)S(1)} collective-permute-done((bf16[10,5,16,128]{3,2,1,0:T(8,128)(2,1)S(1)}, bf16[10,5,16,128]{3,2,1,0:T(8,128)(2,1)S(1)}, u32[]{:S(2)}, u32[]{:S(2)}) %collective-permute-start.39) | collective-permute-done | bytes 204832 | tf_op jit(solution)/shard_map/ppermute | solution.py:88
  108.2 2.4 %collective-permute-done.35.refs_13_ = bf16[10,5,16,128]{3,2,1,0:T(8,128)(2,1)S(1)} collective-permute-done((bf16[10,5,16,128]{3,2,1,0:T(8,128)(2,1)S(1)}, bf16[10,5,16,128]{3,2,1,0:T(8,128)(2,1)S(1)}, u32[]{:S(2)}, u32[]{:S(2)}) %collective-permute-start.35) | collective-permute-done | bytes 204832 | tf_op jit(solution)/shard_map/ppermute | solution.py:88
  121.3 2.8 %collective-permute-done.44.refs_10_ = bf16[10,5,16,128]{3,2,1,0:T(8,128)(2,1)S(1)} collective-permute-done((bf16[10,5,16,128]{3,2,1,0:T(8,128)(2,1)S(1)}, bf16[10,5,16,128]{3,2,1,0:T(8,128)(2,1)S(1)}, u32[]{:S(2)}, u32[]{:S(2)}) %collective-permute-start.44) | collective-permute-done | bytes 204832 | tf_op jit(solution)/shard_map/ppermute | solution.py:88
  127.1 4.1 %forward.3.part = f32[2,176,2560]{2,1,0:T(8,128)S(1)} custom-call(s32[109]{0:T(128)S(1)} %pad_add_fusion.scal, bf16[20,128,384]{2,1,0:T(8,128)(2,1)S(1)} %turn.3.act_t, bf16[2,176,2560]{2,1,0:T(8,128)(2,1)S(1)} %pick.7.kept, bf16[3,176,2560]{2,1,0:T(8,128)(2,1)S(1)} %collective-permute-done.20.sib, bf16[10,5,16,128]{3,2,1,0:T(8,128)(2,1)S(1)} %get-tuple-element.164.refs_0_, ...), custom_call_target="tpu_custom_call" | custom-call | flops 1153433600 | bytes 16777216 | tf_op jit(solution)/shard_map/forward/pallas_call | solution.py:135
  139.5 3.3 %terms.3 = (bf16[10,5,16,128]{3,2,1,0:T(8,128)(2,1)S(1)}, bf16[10,5,16,128]{3,2,1,0:T(8,128)(2,1)S(1)}, bf16[10,5,16,128]{3,2,1,0:T(8,128)(2,1)S(1)}, bf16[10,5,...) custom-call(s32[109]{0:T(128)S(1)} %pad_add_fusion.scal, ...), custom_call_target="tpu_custom_call" | custom-call | flops 1258291200 | bytes 16777216 | tf_op jit(solution)/shard_map/terms/pallas_call | solution.py:135
  147.1 3.7 %collective-permute-done.56.a = bf16[10,5,16,128]{3,2,1,0:T(8,128)(2,1)S(1)} collective-permute-done((bf16[10,5,16,128]{3,2,1,0:T(8,128)(2,1)S(1)}, bf16[10,5,16,128]{3,2,1,0:T(8,128)(2,1)S(1)}, u32[]{:S(2)}, u32[]{:S(2)}) %collective-permute-start.56) | collective-permute-done | bytes 204832 | tf_op jit(solution)/shard_map/ppermute | solution.py:88
  153.1 3.7 %collective-permute-done.53.a = bf16[10,5,16,128]{3,2,1,0:T(8,128)(2,1)S(1)} collective-permute-done((bf16[10,5,16,128]{3,2,1,0:T(8,128)(2,1)S(1)}, bf16[10,5,16,128]{3,2,1,0:T(8,128)(2,1)S(1)}, u32[]{:S(2)}, u32[]{:S(2)}) %collective-permute-start.53) | collective-permute-done | bytes 204832 | tf_op jit(solution)/shard_map/ppermute | solution.py:88
  161.9 3.7 %collective-permute-done.54.a = bf16[10,5,16,128]{3,2,1,0:T(8,128)(2,1)S(1)} collective-permute-done((bf16[10,5,16,128]{3,2,1,0:T(8,128)(2,1)S(1)}, bf16[10,5,16,128]{3,2,1,0:T(8,128)(2,1)S(1)}, u32[]{:S(2)}, u32[]{:S(2)}) %collective-permute-start.54) | collective-permute-done | bytes 204832 | tf_op jit(solution)/shard_map/ppermute | solution.py:88
  170.0 2.7 %collective-permute-done.55.refs_1_ = bf16[10,5,16,128]{3,2,1,0:T(8,128)(2,1)S(1)} collective-permute-done((bf16[10,5,16,128]{3,2,1,0:T(8,128)(2,1)S(1)}, bf16[10,5,16,128]{3,2,1,0:T(8,128)(2,1)S(1)}, u32[]{:S(2)}, u32[]{:S(2)}) %collective-permute-start.55) | collective-permute-done | bytes 204832 | tf_op jit(solution)/shard_map/ppermute | solution.py:88
  (170 shorter events, 102.9 us)
Async XLA Ops:
  5.5 19.9 %collective-permute-start.4 = (bf16[3,176,2560]{2,1,0:T(8,128)(2,1)S(1)}, bf16[3,176,2560]{2,1,0:T(8,128)(2,1)S(1)}, u32[]{:S(2)}, u32[]{:S(2)}) collective-permute-start(bf16[3,176,2560]{2,1,0:T(8,128)(2,1)S(1)} %pick.4.own), channel_id=1, source_target_pairs={{0,1},{1,0},{2,3},{3,2},{4,5},{5,4},{6,7},{7,6},{8,9},{9,8},{10,11... | collective-permute-start | bytes 8110088 | tf_op jit(solution)/shard_map/ppermute | solution.py:74
  5.7 9.0 %collective-permute-start.11 = (bf16[10,5,16,128]{3,2,1,0:T(8,128)(2,1)S(1)}, bf16[10,5,16,128]{3,2,1,0:T(8,128)(2,1)S(1)}, u32[]{:S(2)}, u32[]{:S(2)}) collective-permute-start(bf16[10,5,16,128]{3,2,1,0:T(8,128)(2,1)S(1)} %get-tuple-element.114.refs_7_), channel_id=1, source_target_pairs={{4,0},{5,1},{8,4},{9,5},{12,8},{13,9},{14,12},{15,13},{10,14},{11,... | collective-permute-start | bytes 614408 | tf_op jit(solution)/shard_map/ppermute | solution.py:88
  8.8 12.2 %collective-permute-start.3 = (bf16[10,5,16,128]{3,2,1,0:T(8,128)(2,1)S(1)}, bf16[10,5,16,128]{3,2,1,0:T(8,128)(2,1)S(1)}, u32[]{:S(2)}, u32[]{:S(2)}) collective-permute-start(bf16[10,5,16,128]{3,2,1,0:T(8,128)(2,1)S(1)} %get-tuple-element.114.refs_7_), channel_id=1, source_target_pairs={{0,4},{1,5},{4,8},{5,9},{8,12},{9,13},{12,14},{13,15},{14,10},{15,... | collective-permute-start | bytes 614408 | tf_op jit(solution)/shard_map/ppermute | solution.py:88
  10.8 10.3 %collective-permute-start.5 = (bf16[10,5,16,128]{3,2,1,0:T(8,128)(2,1)S(1)}, bf16[10,5,16,128]{3,2,1,0:T(8,128)(2,1)S(1)}, u32[]{:S(2)}, u32[]{:S(2)}) collective-permute-start(bf16[10,5,16,128]{3,2,1,0:T(8,128)(2,1)S(1)} %get-tuple-element.121.refs_0_), channel_id=1, source_target_pairs={{4,0},{5,1},{8,4},{9,5},{12,8},{13,9},{14,12},{15,13},{10,14},{11,... | collective-permute-start | bytes 614408 | tf_op jit(solution)/shard_map/ppermute | solution.py:88
  14.7 8.8 %collective-permute-start.12 = (bf16[10,5,16,128]{3,2,1,0:T(8,128)(2,1)S(1)}, bf16[10,5,16,128]{3,2,1,0:T(8,128)(2,1)S(1)}, u32[]{:S(2)}, u32[]{:S(2)}) collective-permute-start(bf16[10,5,16,128]{3,2,1,0:T(8,128)(2,1)S(1)} %collective-permute-done.11.refs_8_), channel_id=1, source_target_pairs={{4,0},{5,1},{8,4},{9,5},{12,8},{13,9},{14,12},{15,13},{10,14},{11,... | collective-permute-start | bytes 614408 | tf_op jit(solution)/shard_map/ppermute | solution.py:88
  16.7 10.5 %collective-permute-start.9 = (bf16[10,5,16,128]{3,2,1,0:T(8,128)(2,1)S(1)}, bf16[10,5,16,128]{3,2,1,0:T(8,128)(2,1)S(1)}, u32[]{:S(2)}, u32[]{:S(2)}) collective-permute-start(bf16[10,5,16,128]{3,2,1,0:T(8,128)(2,1)S(1)} %collective-permute-done.8.refs_6_), channel_id=1, source_target_pairs={{0,4},{1,5},{4,8},{5,9},{8,12},{9,13},{12,14},{13,15},{14,10},{15,... | collective-permute-start | bytes 614408 | tf_op jit(solution)/shard_map/ppermute | solution.py:88
  23.4 10.1 %collective-permute-start.13 = (bf16[10,5,16,128]{3,2,1,0:T(8,128)(2,1)S(1)}, bf16[10,5,16,128]{3,2,1,0:T(8,128)(2,1)S(1)}, u32[]{:S(2)}, u32[]{:S(2)}) collective-permute-start(bf16[10,5,16,128]{3,2,1,0:T(8,128)(2,1)S(1)} %collective-permute-done.12.refs_9_), channel_id=1, source_target_pairs={{4,0},{5,1},{8,4},{9,5},{12,8},{13,9},{14,12},{15,13},{10,14},{11,... | collective-permute-start | bytes 614408 | tf_op jit(solution)/shard_map/ppermute | solution.py:88
  29.1 8.8 %collective-permute-start.7 = (bf16[10,5,16,128]{3,2,1,0:T(8,128)(2,1)S(1)}, bf16[10,5,16,128]{3,2,1,0:T(8,128)(2,1)S(1)}, u32[]{:S(2)}, u32[]{:S(2)}) collective-permute-start(bf16[10,5,16,128]{3,2,1,0:T(8,128)(2,1)S(1)} %collective-permute-done.6.refs_2_), channel_id=1, source_target_pairs={{4,0},{5,1},{8,4},{9,5},{12,8},{13,9},{14,12},{15,13},{10,14},{11,... | collective-permute-start | bytes 614408 | tf_op jit(solution)/shard_map/ppermute | solution.py:88
  30.7 8.9 %collective-permute-start.15 = (bf16[10,5,16,128]{3,2,1,0:T(8,128)(2,1)S(1)}, bf16[10,5,16,128]{3,2,1,0:T(8,128)(2,1)S(1)}, u32[]{:S(2)}, u32[]{:S(2)}) collective-permute-start(bf16[10,5,16,128]{3,2,1,0:T(8,128)(2,1)S(1)} %collective-permute-done.14.refs_12_), channel_id=1, source_target_pairs={{0,4},{1,5},{4,8},{5,9},{8,12},{9,13},{12,14},{13,15},{14,10},{15,... | collective-permute-start | bytes 614408 | tf_op jit(solution)/shard_map/ppermute | solution.py:88
  33.5 10.2 %collective-permute-start.17 = (bf16[10,5,16,128]{3,2,1,0:T(8,128)(2,1)S(1)}, bf16[10,5,16,128]{3,2,1,0:T(8,128)(2,1)S(1)}, u32[]{:S(2)}, u32[]{:S(2)}) collective-permute-start(bf16[10,5,16,128]{3,2,1,0:T(8,128)(2,1)S(1)} %collective-permute-done.13.refs_10_), channel_id=1, source_target_pairs={{4,0},{5,1},{8,4},{9,5},{12,8},{13,9},{14,12},{15,13},{10,14},{11,... | collective-permute-start | bytes 614408 | tf_op jit(solution)/shard_map/ppermute | solution.py:88
  47.2 11.6 %collective-permute-start.20 = (bf16[3,176,2560]{2,1,0:T(8,128)(2,1)S(1)}, bf16[3,176,2560]{2,1,0:T(8,128)(2,1)S(1)}, u32[]{:S(2)}, u32[]{:S(2)}) collective-permute-start(bf16[3,176,2560]{2,1,0:T(8,128)(2,1)S(1)} %pick.6.own), channel_id=1, source_target_pairs={{0,1},{1,0},{2,3},{3,2},{4,5},{5,4},{6,7},{7,6},{8,9},{9,8},{10,11... | collective-permute-start | bytes 8110088 | tf_op jit(solution)/shard_map/ppermute | solution.py:74
  57.2 10.3 %collective-permute-start.31 = (bf16[10,5,16,128]{3,2,1,0:T(8,128)(2,1)S(1)}, bf16[10,5,16,128]{3,2,1,0:T(8,128)(2,1)S(1)}, u32[]{:S(2)}, u32[]{:S(2)}) collective-permute-start(bf16[10,5,16,128]{3,2,1,0:T(8,128)(2,1)S(1)} %add.60), channel_id=1, source_target_pairs={{4,0},{5,1},{8,4},{9,5},{12,8},{13,9},{14,12},{15,13},{10,14},{11,... | collective-permute-start | bytes 614408 | tf_op jit(solution)/shard_map/ppermute | solution.py:88
  58.8 10.3 %collective-permute-start.21 = (bf16[10,5,16,128]{3,2,1,0:T(8,128)(2,1)S(1)}, bf16[10,5,16,128]{3,2,1,0:T(8,128)(2,1)S(1)}, u32[]{:S(2)}, u32[]{:S(2)}) collective-permute-start(bf16[10,5,16,128]{3,2,1,0:T(8,128)(2,1)S(1)} %add.53), channel_id=1, source_target_pairs={{0,4},{1,5},{4,8},{5,9},{8,12},{9,13},{12,14},{13,15},{14,10},{15,... | collective-permute-start | bytes 614408 | tf_op jit(solution)/shard_map/ppermute | solution.py:88
  69.7 13.7 %collective-permute-start.34 = (f32[20,5,8,128]{3,2,1,0:T(8,128)S(1)}, f32[20,5,8,128]{3,2,1,0:T(8,128)S(1)}, u32[]{:S(2)}, u32[]{:S(2)}) collective-permute-start(f32[20,5,8,128]{3,2,1,0:T(8,128)S(1)} %get-tuple-element.156), channel_id=1, source_target_pairs={{0,1},{1,0},{2,3},{3,2},{4,5},{5,4},{6,7},{7,6},{8,9},{9,8},{10,11... | collective-permute-start | bytes 1228808 | tf_op jit(solution)/shard_map/ppermute | solution.py:74
  86.3 10.3 %collective-permute-start = (bf16[20,5,16,128]{3,2,1,0:T(8,128)(2,1)}, bf16[20,5,16,128]{3,2,1,0:T(8,128)(2,1)}, u32[]{:S(2)}, u32[]{:S(2)}) collective-permute-start(bf16[20,5,16,128]{3,2,1,0:T(8,128)(2,1)} %param.1), channel_id=1, source_target_pairs={{0,16},{16,0},{1,17},{17,1},{2,18},{18,2},{3,19},{19,3},{4,20},{20... | collective-permute-start | bytes 1228808 | tf_op jit(solution)/shard_map/cond/branch_1_fun/ppermute | solution.py:745
  100.1 10.4 %collective-permute-start.35 = (bf16[10,5,16,128]{3,2,1,0:T(8,128)(2,1)S(1)}, bf16[10,5,16,128]{3,2,1,0:T(8,128)(2,1)S(1)}, u32[]{:S(2)}, u32[]{:S(2)}) collective-permute-start(bf16[10,5,16,128]{3,2,1,0:T(8,128)(2,1)S(1)} %get-tuple-element.162.refs_7_), channel_id=1, source_target_pairs={{0,4},{1,5},{4,8},{5,9},{8,12},{9,13},{12,14},{13,15},{14,10},{15,... | collective-permute-start | bytes 614408 | tf_op jit(solution)/shard_map/ppermute | solution.py:88
  100.6 10.4 %collective-permute-start.36 = (bf16[10,5,16,128]{3,2,1,0:T(8,128)(2,1)S(1)}, bf16[10,5,16,128]{3,2,1,0:T(8,128)(2,1)S(1)}, u32[]{:S(2)}, u32[]{:S(2)}) collective-permute-start(bf16[10,5,16,128]{3,2,1,0:T(8,128)(2,1)S(1)} %get-tuple-element.164.refs_0_), channel_id=1, source_target_pairs={{4,0},{5,1},{8,4},{9,5},{12,8},{13,9},{14,12},{15,13},{10,14},{11,... | collective-permute-start | bytes 614408 | tf_op jit(solution)/shard_map/ppermute | solution.py:88
  106.1 8.8 %collective-permute-start.40 = (bf16[10,5,16,128]{3,2,1,0:T(8,128)(2,1)S(1)}, bf16[10,5,16,128]{3,2,1,0:T(8,128)(2,1)S(1)}, u32[]{:S(2)}, u32[]{:S(2)}) collective-permute-start(bf16[10,5,16,128]{3,2,1,0:T(8,128)(2,1)S(1)} %collective-permute-done.39.refs_6_), channel_id=1, source_target_pairs={{0,4},{1,5},{4,8},{5,9},{8,12},{9,13},{12,14},{13,15},{14,10},{15,... | collective-permute-start | bytes 614408 | tf_op jit(solution)/shard_map/ppermute | solution.py:88
  110.5 8.8 %collective-permute-start.45 = (bf16[10,5,16,128]{3,2,1,0:T(8,128)(2,1)S(1)}, bf16[10,5,16,128]{3,2,1,0:T(8,128)(2,1)S(1)}, u32[]{:S(2)}, u32[]{:S(2)}) collective-permute-start(bf16[10,5,16,128]{3,2,1,0:T(8,128)(2,1)S(1)} %collective-permute-done.35.refs_13_), channel_id=1, source_target_pairs={{0,4},{1,5},{4,8},{5,9},{8,12},{9,13},{12,14},{13,15},{14,10},{15,... | collective-permute-start | bytes 614408 | tf_op jit(solution)/shard_map/ppermute | solution.py:88
  111.0 8.8 %collective-permute-start.37 = (bf16[10,5,16,128]{3,2,1,0:T(8,128)(2,1)S(1)}, bf16[10,5,16,128]{3,2,1,0:T(8,128)(2,1)S(1)}, u32[]{:S(2)}, u32[]{:S(2)}) collective-permute-start(bf16[10,5,16,128]{3,2,1,0:T(8,128)(2,1)S(1)} %collective-permute-done.36.refs_1_), channel_id=1, source_target_pairs={{4,0},{5,1},{8,4},{9,5},{12,8},{13,9},{14,12},{15,13},{10,14},{11,... | collective-permute-start | bytes 614408 | tf_op jit(solution)/shard_map/ppermute | solution.py:88
  116.9 8.8 %collective-permute-start.41 = (bf16[10,5,16,128]{3,2,1,0:T(8,128)(2,1)S(1)}, bf16[10,5,16,128]{3,2,1,0:T(8,128)(2,1)S(1)}, u32[]{:S(2)}, u32[]{:S(2)}) collective-permute-start(bf16[10,5,16,128]{3,2,1,0:T(8,128)(2,1)S(1)} %collective-permute-done.40.refs_5_), channel_id=1, source_target_pairs={{0,4},{1,5},{4,8},{5,9},{8,12},{9,13},{12,14},{13,15},{14,10},{15,... | collective-permute-start | bytes 614408 | tf_op jit(solution)/shard_map/ppermute | solution.py:88
  144.9 11.9 %collective-permute-start.53 = (bf16[10,5,16,128]{3,2,1,0:T(8,128)(2,1)S(1)}, bf16[10,5,16,128]{3,2,1,0:T(8,128)(2,1)S(1)}, u32[]{:S(2)}, u32[]{:S(2)}) collective-permute-start(bf16[10,5,16,128]{3,2,1,0:T(8,128)(2,1)S(1)} %add.63), channel_id=1, source_target_pairs={{0,4},{1,5},{4,8},{5,9},{8,12},{9,13},{12,14},{13,15},{14,10},{15,... | collective-permute-start | bytes 614408 | tf_op jit(solution)/shard_map/ppermute | solution.py:88
  145.5 11.9 %collective-permute-start.63 = (bf16[10,5,16,128]{3,2,1,0:T(8,128)(2,1)S(1)}, bf16[10,5,16,128]{3,2,1,0:T(8,128)(2,1)S(1)}, u32[]{:S(2)}, u32[]{:S(2)}) collective-permute-start(bf16[10,5,16,128]{3,2,1,0:T(8,128)(2,1)S(1)} %add.70), channel_id=1, source_target_pairs={{4,0},{5,1},{8,4},{9,5},{12,8},{13,9},{14,12},{15,13},{10,14},{11,... | collective-permute-start | bytes 614408 | tf_op jit(solution)/shard_map/ppermute | solution.py:88
  159.7 9.0 %collective-permute-start.58 = (bf16[10,5,16,128]{3,2,1,0:T(8,128)(2,1)S(1)}, bf16[10,5,16,128]{3,2,1,0:T(8,128)(2,1)S(1)}, u32[]{:S(2)}, u32[]{:S(2)}) collective-permute-start(bf16[10,5,16,128]{3,2,1,0:T(8,128)(2,1)S(1)} %add.67), channel_id=1, source_target_pairs={{4,0},{5,1},{8,4},{9,5},{12,8},{13,9},{14,12},{15,13},{10,14},{11,... | collective-permute-start | bytes 614408 | tf_op jit(solution)/shard_map/ppermute | solution.py:88
  (49 other events, 389.1 us)
